TPU v7x, 256 devices: a whole 4x4x8 slice. The times are simulated.
256 devices in a mesh: ctx: 32 (over y, x, core), tp: 8 (over z).
Axes of the slice: x: 4, y: 4, z: 8, core: 2. Of those that a mesh axis runs over, the one named last changes fastest.
Arguments:
- token_ids: int32 [8192], P('ctx'), may hold values from 0 to 511
- table: bfloat16 [512, 3, 4096], P(None, None, 'tp'), may hold values from -6 to 6
- filter_raw: float32 [8192, 4096], P('ctx', 'tp'), may hold values from -6 to 6
- w_out: bfloat16 [4096, 4096], P('tp'), may hold values from -0.09375 to 0.09375
- cotangent: bfloat16 [8192, 4096], P('ctx', 'tp'), may hold values from -6 to 6
Outputs:
- output: bfloat16 [8192, 4096], P('ctx', 'tp')
- grad_filter: float32 [8192, 4096], P('ctx', 'tp')
- grad_table: float32 [512, 3, 4096], P('ctx', None, 'tp')
All inputs are finite; a program needn't handle non-finite values.
Results may differ from a plain program's by a relative error of at most 0.019.
Values may be sent and summed in bfloat16 or wider, within the bound.
No kernel may reach another device: no remote copies, remote signals or barrier semaphores. Data moves between devices by JAX's collectives and lax.ppermute only.
A program may use at most 128 MiB of HBM per device.

v0:
```python
import math

import jax
import jax.numpy as jnp
from jax import lax
from jax.sharding import PartitionSpec as P

exact_mode = lax.Precision.HIGHEST


def phases(row_index, col_index, period):
    product = row_index[:, None] * col_index[None, :] % period
    return product.astype(jnp.float32) * (2.0 * math.pi / period)


def contract(pattern, leading, trailing):
    return jnp.einsum(
        pattern, leading, trailing, precision=exact_mode, preferred_element_type=jnp.float32
    )


def widen(table_two):
    return table_two[:, :, None]


def section_one(pieces, column_start, period):
    outer_len = pieces.shape[0]
    inner_len = pieces.shape[1]
    pattern = "djc,dk->kjc"
    outer = phases(
        lax.iota(jnp.int32, outer_len), lax.iota(jnp.int32, 2 * outer_len), 2 * outer_len
    )
    real_part = contract(pattern, pieces, jnp.cos(outer))
    imag_part = -contract(pattern, pieces, jnp.sin(outer))
    twiddle = widen(
        phases(
            lax.iota(jnp.int32, 2 * outer_len),
            column_start + lax.iota(jnp.int32, inner_len),
            period,
        )
    )
    cosine_table = jnp.cos(twiddle)
    sine_table = jnp.sin(twiddle)
    return (
        real_part * cosine_table + imag_part * sine_table,
        imag_part * cosine_table - real_part * sine_table,
    )


def section_two(real_part, imag_part):
    length = real_part.shape[1]
    pattern = "kjc,jm->kmc"
    angles = phases(lax.iota(jnp.int32, length), lax.iota(jnp.int32, length), length)
    cosine_table = jnp.cos(angles)
    sine_table = jnp.sin(angles)
    new_real = contract(pattern, real_part, cosine_table) + contract(pattern, imag_part, sine_table)
    new_imag = contract(pattern, imag_part, cosine_table) - contract(pattern, real_part, sine_table)
    return (new_real, new_imag)


def section_two_inverse(real_part, imag_part, row_start, period):
    outer_len = real_part.shape[0]
    length = real_part.shape[1]
    pattern = "kmc,mj->kjc"
    angles = phases(lax.iota(jnp.int32, length), lax.iota(jnp.int32, length), length)
    cosine_table = jnp.cos(angles)
    sine_table = jnp.sin(angles)
    new_real = contract(pattern, real_part, cosine_table) - contract(pattern, imag_part, sine_table)
    new_imag = contract(pattern, imag_part, cosine_table) + contract(pattern, real_part, sine_table)
    twiddle = widen(
        phases(row_start + lax.iota(jnp.int32, outer_len), lax.iota(jnp.int32, length), period)
    )
    twist_cos = jnp.cos(twiddle)
    twist_sin = jnp.sin(twiddle)
    return (
        new_real * twist_cos - new_imag * twist_sin,
        new_imag * twist_cos + new_real * twist_sin,
    )


def section_one_inverse(real_part, imag_part, period):
    outer_len = real_part.shape[0] // 2
    pattern = "kjc,dk->djc"
    outer = phases(
        lax.iota(jnp.int32, outer_len), lax.iota(jnp.int32, 2 * outer_len), 2 * outer_len
    )
    summed = contract(pattern, real_part, jnp.cos(outer)) - contract(
        pattern, imag_part, jnp.sin(outer)
    )
    return summed / period


def shards(token_ids, table, filter_raw, w_out, cotangent):
    row_count = token_ids.shape[0]
    device_count = lax.axis_size("ctx")
    length = row_count * device_count
    period = 2 * length
    position = lax.axis_index("ctx")

    def to_spectrum(signal):
        pieces = lax.all_to_all(signal[None], "ctx", split_axis=1, concat_axis=0, tiled=True)
        real_part, imag_part = section_one(pieces, position * (row_count // device_count), period)
        real_part, imag_part = (
            lax.all_to_all(real_part, "ctx", split_axis=0, concat_axis=1, tiled=True),
            lax.all_to_all(imag_part, "ctx", split_axis=0, concat_axis=1, tiled=True),
        )
        return section_two(real_part, imag_part)

    def from_spectrum(real_part, imag_part):
        real_part, imag_part = section_two_inverse(real_part, imag_part, 2 * position, period)
        real_part, imag_part = (
            lax.all_to_all(real_part, "ctx", split_axis=1, concat_axis=0, tiled=True),
            lax.all_to_all(imag_part, "ctx", split_axis=1, concat_axis=0, tiled=True),
        )
        signal = section_one_inverse(real_part, imag_part, period)
        return lax.all_to_all(signal, "ctx", split_axis=0, concat_axis=1, tiled=True)[0]

    embedded = jnp.take(table, token_ids, axis=0)
    query_part = embedded[:, 0].astype(jnp.float32)
    key_part = embedded[:, 1].astype(jnp.float32)
    value_part = embedded[:, 2].astype(jnp.float32)
    gated_input = key_part * value_part
    filter_scale = 1.0 / math.sqrt(length)
    filter_time = filter_raw * filter_scale
    input_real, input_imag = to_spectrum(gated_input)
    filter_real, filter_imag = to_spectrum(filter_time)
    causal = from_spectrum(
        input_real * filter_real - input_imag * filter_imag,
        input_real * filter_imag + input_imag * filter_real,
    )
    mixed_rows = (query_part * causal).astype(jnp.bfloat16)
    partial_out = jnp.dot(mixed_rows, w_out, preferred_element_type=jnp.float32)
    output = lax.psum_scatter(
        partial_out.astype(jnp.bfloat16), "tp", scatter_dimension=1, tiled=True
    )
    back_grad = lax.dot_general(
        lax.all_gather(cotangent, "tp", axis=1, tiled=True),
        w_out,
        (((1,), (1,)), ((), ())),
        preferred_element_type=jnp.float32,
    )
    causal_grad = back_grad * query_part
    query_grad = back_grad * causal
    grad_real, grad_imag = to_spectrum(causal_grad)
    gated_grad = from_spectrum(
        filter_real * grad_real + filter_imag * grad_imag,
        filter_real * grad_imag - filter_imag * grad_real,
    )
    filter_grad = from_spectrum(
        input_real * grad_real + input_imag * grad_imag,
        input_real * grad_imag - input_imag * grad_real,
    )
    grad_filter = filter_grad * filter_scale
    activation = jnp.stack(
        [query_grad, gated_grad * value_part, gated_grad * key_part], axis=1
    ).astype(jnp.bfloat16)
    flattened = activation.reshape(row_count, -1)
    vocab_rows = table.shape[0] // device_count
    labels = lax.iota(jnp.int32, vocab_rows * lax.axis_size("ctx"))
    onehot = (labels[:, None] == token_ids[None, :]).astype(jnp.bfloat16)
    grad_rows = lax.psum_scatter(
        jnp.dot(onehot, flattened, preferred_element_type=jnp.float32).astype(jnp.bfloat16),
        "ctx",
        scatter_dimension=0,
        tiled=True,
    ).astype(jnp.float32)
    return (output, grad_filter, grad_rows.reshape(vocab_rows, 3, -1))


def solution(mesh):
    return jax.shard_map(
        shards,
        mesh=mesh,
        in_specs=(P("ctx"), P(None, None, "tp"), P("ctx", "tp"), P("tp", None), P("ctx", "tp")),
        out_specs=(P("ctx", "tp"), P("ctx", "tp"), P("ctx", None, "tp")),
        check_vma=False,
    )
```

profile of v0, /device:TPU:6, one launch (start us, length us, event | category | flops | bytes accessed | tf_op | source)
XLA Modules:
  0.0 528.3 jit_solution(7343315810524735823)
XLA Ops:
  13.4 7.6 %all-to-all-start = ((f32[1,256,512]{2,0,1:T(1,128)}), f32[1,256,512]{2,0,1:T(1,128)S(1)}, u32[]{:S(2)}, u32[]{:S(2)}) async-start(f32[1,256,512]{2,0,1:T(1,128)} %copy.81), calls=%async_computation | async-start | bytes 1048576 | tf_op jit(solution)/shard_map/all_to_all | solution.py:101
  22.2 8.1 %all-to-all-done = f32[1,256,512]{2,0,1:T(1,128)S(1)} async-done(((f32[1,256,512]{2,0,1:T(1,128)}), f32[1,256,512]{2,0,1:T(1,128)S(1)}, u32[]{:S(2)}, u32[]{:S(2)}) %all-to-all-start) | async-done | bytes 524320 | tf_op jit(solution)/shard_map/all_to_all | solution.py:101
  36.7 9.3 %all-to-all-done.3 = f32[1,256,512]{2,0,1:T(1,128)S(1)} async-done(((f32[1,256,512]{2,0,1:T(1,128)}), f32[1,256,512]{2,0,1:T(1,128)S(1)}, u32[]{:S(2)}, u32[]{:S(2)}) %all-to-all-start.3) | async-done | bytes 524320 | tf_op jit(solution)/shard_map/all_to_all | solution.py:101
  59.7 7.7 %all-to-all-start.9 = ((f32[1,256,512]{2,0,1:T(1,128)}), f32[1,256,512]{2,0,1:T(1,128)S(1)}, u32[]{:S(2)}, u32[]{:S(2)}) async-start(f32[1,256,512]{2,0,1:T(1,128)} %copy.99), calls=%async_computation.10 | async-start | bytes 1048576 | tf_op jit(solution)/shard_map/all_to_all | solution.py:101
  93.0 13.1 %all-to-all-done.1 = f32[64,8,512]{2,1,0:T(8,128)S(1)} async-done(((f32[64,8,512]{2,1,0:T(8,128)}), f32[64,8,512]{2,1,0:T(8,128)S(1)}, u32[]{:S(2)}, u32[]{:S(2)}) %all-to-all-start.1) | async-done | bytes 1048608 | tf_op jit(solution)/shard_map/all_to_all | solution.py:104
  114.3 13.1 %all-to-all-done.2 = f32[64,8,512]{2,1,0:T(8,128)S(1)} async-done(((f32[64,8,512]{2,1,0:T(8,128)}), f32[64,8,512]{2,1,0:T(8,128)S(1)}, u32[]{:S(2)}, u32[]{:S(2)}) %all-to-all-start.2) | async-done | bytes 1048608 | tf_op jit(solution)/shard_map/all_to_all | solution.py:105
  136.7 11.9 %all-to-all-done.10 = f32[64,8,512]{2,1,0:T(8,128)S(1)} async-done(((f32[64,8,512]{2,1,0:T(8,128)}), f32[64,8,512]{2,1,0:T(8,128)S(1)}, u32[]{:S(2)}, u32[]{:S(2)}) %all-to-all-start.10) | async-done | bytes 1048608 | tf_op jit(solution)/shard_map/all_to_all | solution.py:104
  148.6 7.2 %all-to-all-start.4 = ((f32[64,8,512]{2,1,0:T(8,128)}), f32[64,8,512]{2,1,0:T(8,128)}, u32[]{:S(2)}, u32[]{:S(2)}) async-start(f32[64,8,512]{2,1,0:T(8,128)} %copy.90), calls=%async_computation.4 | async-start | bytes 2097152 | tf_op jit(solution)/shard_map/all_to_all | solution.py:104
  160.5 10.1 %all-to-all-done.4 = f32[64,8,512]{2,1,0:T(8,128)} async-done(((f32[64,8,512]{2,1,0:T(8,128)}), f32[64,8,512]{2,1,0:T(8,128)}, u32[]{:S(2)}, u32[]{:S(2)}) %all-to-all-start.4) | async-done | bytes 1048608 | tf_op jit(solution)/shard_map/all_to_all | solution.py:104
  170.6 7.6 %all-to-all-start.11 = ((f32[64,8,512]{2,1,0:T(8,128)}), f32[64,8,512]{2,1,0:T(8,128)}, u32[]{:S(2)}, u32[]{:S(2)}) async-start(f32[64,8,512]{2,1,0:T(8,128)} %copy.104), calls=%async_computation.12 | async-start | bytes 2097152 | tf_op jit(solution)/shard_map/all_to_all | solution.py:105
  193.0 7.4 %all-to-all-start.5 = ((f32[64,8,512]{2,1,0:T(8,128)}), f32[64,8,512]{2,1,0:T(8,128)}, u32[]{:S(2)}, u32[]{:S(2)}) async-start(f32[64,8,512]{2,1,0:T(8,128)} %copy.92), calls=%async_computation.5 | async-start | bytes 2097152 | tf_op jit(solution)/shard_map/all_to_all | solution.py:105
  257.3 7.2 %all-to-all-start.15 = ((f32[2,256,512]{2,0,1:T(2,128)}), f32[2,256,512]{2,0,1:T(2,128)}, u32[]{:S(2)}, u32[]{:S(2)}) async-start(f32[2,256,512]{2,0,1:T(2,128)} %copy.111), calls=%async_computation.16 | async-start | bytes 2097152 | tf_op jit(solution)/shard_map/all_to_all | solution.py:112
  267.6 11.7 %all-to-all-done.15 = f32[2,256,512]{2,0,1:T(2,128)} async-done(((f32[2,256,512]{2,0,1:T(2,128)}), f32[2,256,512]{2,0,1:T(2,128)}, u32[]{:S(2)}, u32[]{:S(2)}) %all-to-all-start.15) | async-done | bytes 1048608 | tf_op jit(solution)/shard_map/all_to_all | solution.py:112
  289.6 11.7 %all-to-all-done.16 = f32[2,256,512]{2,0,1:T(2,128)} async-done(((f32[2,256,512]{2,0,1:T(2,128)}), f32[2,256,512]{2,0,1:T(2,128)}, u32[]{:S(2)}, u32[]{:S(2)}) %all-to-all-start.16) | async-done | bytes 1048608 | tf_op jit(solution)/shard_map/all_to_all | solution.py:113
  311.6 11.7 %all-to-all-done.6 = f32[2,256,512]{2,0,1:T(2,128)} async-done(((f32[2,256,512]{2,0,1:T(2,128)}), f32[2,256,512]{2,0,1:T(2,128)}, u32[]{:S(2)}, u32[]{:S(2)}) %all-to-all-start.6) | async-done | bytes 1048608 | tf_op jit(solution)/shard_map/all_to_all | solution.py:112
  323.3 7.6 %all-to-all-start.7 = ((f32[2,256,512]{2,0,1:T(2,128)}), f32[2,256,512]{2,0,1:T(2,128)}, u32[]{:S(2)}, u32[]{:S(2)}) async-start(f32[2,256,512]{2,0,1:T(2,128)} %copy.96), calls=%async_computation.7 | async-start | bytes 2097152 | tf_op jit(solution)/shard_map/all_to_all | solution.py:113
  351.3 7.5 %all-to-all-start.17 = ((f32[32,8,512]{2,1,0:T(8,128)}), f32[32,8,512]{2,1,0:T(8,128)S(1)}, u32[]{:S(2)}, u32[]{:S(2)}) async-start(f32[32,8,512]{2,1,0:T(8,128)} %copy.115), calls=%async_computation.18 | async-start | bytes 1048576 | tf_op jit(solution)/shard_map/all_to_all | solution.py:116
  368.2 7.4 %all-to-all-start.8 = ((f32[32,8,512]{2,1,0:T(8,128)}), f32[32,8,512]{2,1,0:T(8,128)}, u32[]{:S(2)}, u32[]{:S(2)}) async-start(f32[32,8,512]{2,1,0:T(8,128)} %copy.98), calls=%async_computation.8 | async-start | bytes 1048576 | tf_op jit(solution)/shard_map/all_to_all | solution.py:116
  376.6 8.4 %all-to-all-done.8 = f32[32,8,512]{2,1,0:T(8,128)} async-done(((f32[32,8,512]{2,1,0:T(8,128)}), f32[32,8,512]{2,1,0:T(8,128)}, u32[]{:S(2)}, u32[]{:S(2)}) %all-to-all-start.8) | async-done | bytes 524320 | tf_op jit(solution)/shard_map/all_to_all | solution.py:116
  408.8 12.9 %all-to-all-done.12 = f32[2,256,512]{2,0,1:T(2,128)S(1)} async-done(((f32[2,256,512]{2,0,1:T(2,128)}), f32[2,256,512]{2,0,1:T(2,128)S(1)}, u32[]{:S(2)}, u32[]{:S(2)}) %all-to-all-start.12) | async-done | bytes 1048608 | tf_op jit(solution)/shard_map/all_to_all | solution.py:112
  431.5 11.4 %all-to-all-done.13 = f32[2,256,512]{2,0,1:T(2,128)S(1)} async-done(((f32[2,256,512]{2,0,1:T(2,128)}), f32[2,256,512]{2,0,1:T(2,128)S(1)}, u32[]{:S(2)}, u32[]{:S(2)}) %all-to-all-start.13) | async-done | bytes 1048608 | tf_op jit(solution)/shard_map/all_to_all | solution.py:113
  448.0 15.4 %all_to_all.279 = f32[32,8,512]{2,1,0:T(8,128)S(1)} all-to-all(f32[32,8,512]{2,1,0:T(8,128)S(1)} %copy.110), channel_id=1, replica_groups=mesh['ctx'=32,'tp'=8] {'ctx'}, dimensions={0} | all-to-all | bytes 1048576 | tf_op jit(solution)/shard_map/all_to_all | solution.py:116
  464.3 11.9 %reduce-scatter.5.cloned.1.call-done = bf16[16,1536]{1,0:T(8,128)(2,1)} async-done(((bf16[512,1536]{1,0:T(8,128)(2,1)}), bf16[16,1536]{1,0:T(8,128)(2,1)}) %reduce-scatter.5.cloned.1.call-update) | async-done | bytes 49168 | tf_op jit(solution)/shard_map/reduce_scatter | solution.py:161
  477.7 43.6 %reduce-scatter.3.cloned.1.call-done = bf16[256,512]{1,0:T(8,128)(2,1)} async-done(((bf16[256,4096]{1,0:T(8,128)(2,1)}), bf16[256,512]{1,0:T(8,128)(2,1)}) %reduce-scatter.3.cloned.1.call-update) | async-done | bytes 262160 | tf_op jit(solution)/shard_map/reduce_scatter | solution.py:133
  (153 shorter events, 241.7 us)
Async XLA Ops:
  7.2 46.9 %all-gather.2.cloned.1.call-start = ((), (), s32[]{:S(2)}) async-start(), calls=%async_computation.21 | async-start | bytes 2359296 | tf_op jit(solution)/shard_map/all_gather | solution.py:137
  12.0 46.3 %copy-start.2 = (bf16[256,3,512]{2,0,1:T(8,128)(2,1)}, bf16[256,3,512]{2,0,1:T(8,128)(2,1)S(1)}, u32[]{:S(2)}) copy-start(bf16[256,3,512]{2,0,1:T(8,128)(2,1)S(1)} %broadcast_select_fusion) | copy-start | bytes 2359300
  13.4 16.9 %all-to-all-start = ((f32[1,256,512]{2,0,1:T(1,128)}), f32[1,256,512]{2,0,1:T(1,128)S(1)}, u32[]{:S(2)}, u32[]{:S(2)}) async-start(f32[1,256,512]{2,0,1:T(1,128)} %copy.81), calls=%async_computation | async-start | bytes 1048576 | tf_op jit(solution)/shard_map/all_to_all | solution.py:101
  30.3 15.7 %all-to-all-start.3 = ((f32[1,256,512]{2,0,1:T(1,128)}), f32[1,256,512]{2,0,1:T(1,128)S(1)}, u32[]{:S(2)}, u32[]{:S(2)}) async-start(f32[1,256,512]{2,0,1:T(1,128)} %broadcast_in_dim.19), calls=%async_computation.3 | async-start | bytes 1048576 | tf_op jit(solution)/shard_map/all_to_all | solution.py:101
  58.2 11.5 %copy-start.18 = (f32[256,512]{1,0:T(8,128)}, f32[256,512]{1,0:T(8,128)S(1)}, u32[]{:S(2)}) copy-start(f32[256,512]{1,0:T(8,128)S(1)} %fusion.323) | copy-start | bytes 1572868
  59.7 17.1 %all-to-all-start.9 = ((f32[1,256,512]{2,0,1:T(1,128)}), f32[1,256,512]{2,0,1:T(1,128)S(1)}, u32[]{:S(2)}, u32[]{:S(2)}) async-start(f32[1,256,512]{2,0,1:T(1,128)} %copy.99), calls=%async_computation.10 | async-start | bytes 1048576 | tf_op jit(solution)/shard_map/all_to_all | solution.py:101
  85.2 20.9 %all-to-all-start.1 = ((f32[64,8,512]{2,1,0:T(8,128)}), f32[64,8,512]{2,1,0:T(8,128)S(1)}, u32[]{:S(2)}, u32[]{:S(2)}) async-start(f32[64,8,512]{2,1,0:T(8,128)} %copy.84), calls=%async_computation.1 | async-start | bytes 2097152 | tf_op jit(solution)/shard_map/all_to_all | solution.py:104
  91.4 21.3 %copy-start.6 = (f32[64,8,512]{2,0,1:T(8,128)S(1)}, f32[64,8,512]{2,0,1:T(8,128)}, u32[]{:S(2)}) copy-start(f32[64,8,512]{2,0,1:T(8,128)} %get-tuple-element.22) | copy-start | bytes 3145732
  106.1 21.3 %all-to-all-start.2 = ((f32[64,8,512]{2,1,0:T(8,128)}), f32[64,8,512]{2,1,0:T(8,128)S(1)}, u32[]{:S(2)}, u32[]{:S(2)}) async-start(f32[64,8,512]{2,1,0:T(8,128)} %copy.86), calls=%async_computation.2 | async-start | bytes 2097152 | tf_op jit(solution)/shard_map/all_to_all | solution.py:105
  127.3 21.3 %all-to-all-start.10 = ((f32[64,8,512]{2,1,0:T(8,128)}), f32[64,8,512]{2,1,0:T(8,128)S(1)}, u32[]{:S(2)}, u32[]{:S(2)}) async-start(f32[64,8,512]{2,1,0:T(8,128)} %copy.102), calls=%async_computation.11 | async-start | bytes 2097152 | tf_op jit(solution)/shard_map/all_to_all | solution.py:104
  148.6 22.0 %all-to-all-start.4 = ((f32[64,8,512]{2,1,0:T(8,128)}), f32[64,8,512]{2,1,0:T(8,128)}, u32[]{:S(2)}, u32[]{:S(2)}) async-start(f32[64,8,512]{2,1,0:T(8,128)} %copy.90), calls=%async_computation.4 | async-start | bytes 2097152 | tf_op jit(solution)/shard_map/all_to_all | solution.py:104
  170.6 22.4 %all-to-all-start.11 = ((f32[64,8,512]{2,1,0:T(8,128)}), f32[64,8,512]{2,1,0:T(8,128)}, u32[]{:S(2)}, u32[]{:S(2)}) async-start(f32[64,8,512]{2,1,0:T(8,128)} %copy.104), calls=%async_computation.12 | async-start | bytes 2097152 | tf_op jit(solution)/shard_map/all_to_all | solution.py:105
  193.0 22.0 %all-to-all-start.5 = ((f32[64,8,512]{2,1,0:T(8,128)}), f32[64,8,512]{2,1,0:T(8,128)}, u32[]{:S(2)}, u32[]{:S(2)}) async-start(f32[64,8,512]{2,1,0:T(8,128)} %copy.92), calls=%async_computation.5 | async-start | bytes 2097152 | tf_op jit(solution)/shard_map/all_to_all | solution.py:105
  257.3 22.0 %all-to-all-start.15 = ((f32[2,256,512]{2,0,1:T(2,128)}), f32[2,256,512]{2,0,1:T(2,128)}, u32[]{:S(2)}, u32[]{:S(2)}) async-start(f32[2,256,512]{2,0,1:T(2,128)} %copy.111), calls=%async_computation.16 | async-start | bytes 2097152 | tf_op jit(solution)/shard_map/all_to_all | solution.py:112
  279.3 22.0 %all-to-all-start.16 = ((f32[2,256,512]{2,0,1:T(2,128)}), f32[2,256,512]{2,0,1:T(2,128)}, u32[]{:S(2)}, u32[]{:S(2)}) async-start(f32[2,256,512]{2,0,1:T(2,128)} %copy.113), calls=%async_computation.17 | async-start | bytes 2097152 | tf_op jit(solution)/shard_map/all_to_all | solution.py:113
  301.3 22.0 %all-to-all-start.6 = ((f32[2,256,512]{2,0,1:T(2,128)}), f32[2,256,512]{2,0,1:T(2,128)}, u32[]{:S(2)}, u32[]{:S(2)}) async-start(f32[2,256,512]{2,0,1:T(2,128)} %copy.94), calls=%async_computation.6 | async-start | bytes 2097152 | tf_op jit(solution)/shard_map/all_to_all | solution.py:112
  323.3 28.1 %all-to-all-start.7 = ((f32[2,256,512]{2,0,1:T(2,128)}), f32[2,256,512]{2,0,1:T(2,128)}, u32[]{:S(2)}, u32[]{:S(2)}) async-start(f32[2,256,512]{2,0,1:T(2,128)} %copy.96), calls=%async_computation.7 | async-start | bytes 2097152 | tf_op jit(solution)/shard_map/all_to_all | solution.py:113
  351.3 16.9 %all-to-all-start.17 = ((f32[32,8,512]{2,1,0:T(8,128)}), f32[32,8,512]{2,1,0:T(8,128)S(1)}, u32[]{:S(2)}, u32[]{:S(2)}) async-start(f32[32,8,512]{2,1,0:T(8,128)} %copy.115), calls=%async_computation.18 | async-start | bytes 1048576 | tf_op jit(solution)/shard_map/all_to_all | solution.py:116
  368.2 16.9 %all-to-all-start.8 = ((f32[32,8,512]{2,1,0:T(8,128)}), f32[32,8,512]{2,1,0:T(8,128)}, u32[]{:S(2)}, u32[]{:S(2)}) async-start(f32[32,8,512]{2,1,0:T(8,128)} %copy.98), calls=%async_computation.8 | async-start | bytes 1048576 | tf_op jit(solution)/shard_map/all_to_all | solution.py:116
  375.7 100.5 %reduce-scatter.5.cloned.1.call-start = ((), (), s32[]{:S(2)}) async-start(), calls=%async_computation.22 | async-start | bytes 1622016 | tf_op jit(solution)/shard_map/reduce_scatter | solution.py:161
  393.6 127.7 %reduce-scatter.3.cloned.1.call-start = ((), (), s32[]{:S(2)}) async-start(), calls=%async_computation.20 | async-start | bytes 2359296 | tf_op jit(solution)/shard_map/reduce_scatter | solution.py:133
  400.7 21.0 %all-to-all-start.12 = ((f32[2,256,512]{2,0,1:T(2,128)}), f32[2,256,512]{2,0,1:T(2,128)S(1)}, u32[]{:S(2)}, u32[]{:S(2)}) async-start(f32[2,256,512]{2,0,1:T(2,128)} %copy.106), calls=%async_computation.13 | async-start | bytes 2097152 | tf_op jit(solution)/shard_map/all_to_all | solution.py:112
  421.7 21.3 %all-to-all-start.13 = ((f32[2,256,512]{2,0,1:T(2,128)}), f32[2,256,512]{2,0,1:T(2,128)S(1)}, u32[]{:S(2)}, u32[]{:S(2)}) async-start(f32[2,256,512]{2,0,1:T(2,128)} %copy.108), calls=%async_computation.14 | async-start | bytes 2097152 | tf_op jit(solution)/shard_map/all_to_all | solution.py:113
  447.0 74.3 %copy-start.1 = (bf16[512,3,512]{2,0,1:T(8,128)(2,1)S(1)}, bf16[512,3,512]{2,0,1:T(8,128)(2,1)}, u32[]{:S(2)}) copy-start(bf16[512,3,512]{2,0,1:T(8,128)(2,1)} %param.6) | copy-start | bytes 4718596
  (17 other events, 71.2 us)
Sparse Core Ops, SparseCore 0:
  9.8 44.2 all-gather.1
  393.7 82.4 reduce-scatter.4
  479.3 41.9 reduce-scatter.2
where the time goes:
time: 538 us; the launch traced here: 528 us
  waiting for transfers between devices  201 us (37%)
  starting transfers between devices  120 us (22%)
  matrix products  101 us (19%)
  local copies, waits for them, and re-layouts  68.2 us (13%)
  blocking collectives  15.4 us (3%)
  between operations  14.9 us (3%)
  other arithmetic  7.14 us (1%)
    dot_general x36, matrix products, contract(): jnp.einsum(pattern, leading, trailing, precision=exact_mode, preferred_el...  89.3 us
    reduce_scatter x1, waiting for transfers between devices, shards(): lax.psum_scatter(partial_out.astype(jnp.bfloat16), 'tp', scatter_dimensio...  43.6 us
    all_to_all x3, waiting for transfers between devices, from_spectrum(): lax.all_to_all(real_part, 'ctx', split_axis=1, concat_axis=0, tiled=True)  36.3 us
    all_to_all x3, waiting for transfers between devices, to_spectrum(): lax.all_to_all(real_part, 'ctx', split_axis=0, concat_axis=1, tiled=True)  35 us
    all_to_all x3, waiting for transfers between devices, from_spectrum(): lax.all_to_all(imag_part, 'ctx', split_axis=1, concat_axis=0, tiled=True)  23.1 us
    all_to_all x3, waiting for transfers between devices, to_spectrum(): lax.all_to_all(signal[None], 'ctx', split_axis=1, concat_axis=0, tiled=True)  22.1 us
    all_to_all x3, starting transfers between devices, to_spectrum(): lax.all_to_all(imag_part, 'ctx', split_axis=0, concat_axis=1, tiled=True)  21.6 us
    all_to_all x3, starting transfers between devices, to_spectrum(): lax.all_to_all(signal[None], 'ctx', split_axis=1, concat_axis=0, tiled=True)  21.5 us
  transfers between devices with their start and end apart: 20, of which 18 were waited for; matrix products, arithmetic and copies ran while one was open for 18% of the time, Pallas kernels for 0%

commit v1 on v0

v1 whole, which is shorter than its diff:
```python
import functools
import math

import jax
import jax.numpy as jnp
import ml_dtypes
import numpy as np
from jax import lax
from jax.experimental import pallas as pl
from jax.experimental.pallas import tpu as pltpu
from jax.sharding import PartitionSpec as P

BF = jnp.bfloat16
F32 = jnp.float32


def split_np(values):
    high = values.astype(np.float32).astype(ml_dtypes.bfloat16)
    low = (values - high.astype(np.float64)).astype(np.float32).astype(ml_dtypes.bfloat16)
    return high, low


@functools.lru_cache(maxsize=None)
def tables(blocks, chans, rows):
    period = 2 * blocks * rows
    s = np.arange(blocks, dtype=np.float64)
    r = np.arange(rows, dtype=np.float64)
    odd = np.arange(blocks, dtype=np.float64) + 0.5
    outer = 2 * np.pi * odd[:, None] * s[None, :] / (2 * blocks)
    eye = np.eye(chans)
    real = np.einsum("ks,cd->cksd", np.cos(outer), eye).reshape(chans * blocks, blocks * chans)
    imag = np.einsum("ks,cd->cksd", -np.sin(outer), eye).reshape(chans * blocks, blocks * chans)
    first = np.concatenate([real, imag], axis=0)
    inner = 2 * np.pi * (np.outer(r, r) % rows) / rows
    cosine, sine = np.cos(inner), np.sin(inner)
    second = np.block([[cosine, -sine], [sine, cosine]])
    twist = 2 * np.pi * odd[:, None] * r[None, :] / period
    return (
        split_np(first),
        split_np(second),
        split_np(second.T.copy()),
        split_np(first.T * (2.0 / period)),
        np.cos(twist).astype(np.float32),
        np.sin(twist).astype(np.float32),
    )


def split(values):
    high = values.astype(BF)
    return high, (values - high.astype(F32)).astype(BF)


def mm(left, right):
    return jnp.dot(left, right, preferred_element_type=F32)


def twiddle(real, imag, cos_ref, sin_ref, sign):
    rows, lanes = real.shape
    blocks = cos_ref.shape[0]
    shape = (rows // blocks, blocks, lanes)
    cosine = cos_ref[...][None]
    sine = sin_ref[...][None] * sign
    real = real.reshape(shape)
    imag = imag.reshape(shape)
    return (
        (real * cosine + imag * sine).reshape(rows, lanes),
        (imag * cosine - real * sine).reshape(rows, lanes),
    )


def forward(high, low, first, second, cos_ref, sin_ref):
    first_high, first_low = first
    second_high, second_low = second
    stage = mm(first_high[...], high) + mm(first_low[...], high)
    if low is not None:
        stage = stage + mm(first_high[...], low)
    half = stage.shape[0] // 2
    real, imag = twiddle(stage[:half], stage[half:], cos_ref, sin_ref, 1.0)
    high, low = split(jnp.concatenate([real, imag], axis=1))
    return mm(high, second_high[...]) + mm(low, second_high[...]) + mm(high, second_low[...])


def inverse(spectrum, third, fourth, cos_ref, sin_ref):
    third_high, third_low = third
    fourth_high, fourth_low = fourth
    high, low = split(spectrum)
    stage = mm(high, third_high[...]) + mm(low, third_high[...]) + mm(high, third_low[...])
    half = stage.shape[1] // 2
    real, imag = twiddle(stage[:, :half], stage[:, half:], cos_ref, sin_ref, -1.0)
    high, low = split(jnp.concatenate([real, imag], axis=0))
    return mm(fourth_high[...], high) + mm(fourth_high[...], low) + mm(fourth_low[...], high)


def embed_kernel(ids_ref, tab_ref, q_ref, k_ref, v_ref):
    blocks, rows = ids_ref.shape
    chans = tab_ref.shape[0] // 3
    vocab = tab_ref.shape[1]
    labels = lax.broadcasted_iota(jnp.int32, (vocab, rows), 0)

    def body(s, carry):
        onehot = (labels == ids_ref[pl.ds(s, 1), :]).astype(F32).astype(BF)
        picked = mm(tab_ref[...], onehot).astype(BF)
        place = pl.ds(pl.multiple_of(s * chans, chans), chans)
        q_ref[place, :] = picked[:chans]
        k_ref[place, :] = picked[chans : 2 * chans]
        v_ref[place, :] = picked[2 * chans :]
        return carry

    lax.fori_loop(0, blocks, body, 0)


def input_kernel(k_ref, v_ref, first_high, first_low, second_high, second_low, cos_ref, sin_ref, spec_ref):
    gated = k_ref[...].astype(F32) * v_ref[...].astype(F32)
    high, low = split(gated)
    spec_ref[...] = forward(
        high, low, (first_high, first_low), (second_high, second_low), cos_ref, sin_ref
    )


def causal_kernel(
    scale, f_ref, q_ref, gated_ref,
    first_high, first_low, second_high, second_low,
    third_high, third_low, fourth_high, fourth_low, cos_ref, sin_ref,
    spec_ref, causal_ref, mixed_ref,
):
    spec = forward(
        f_ref[...], None, (first_high, first_low), (second_high, second_low), cos_ref, sin_ref
    ) * scale
    spec_ref[...] = spec
    half = spec.shape[1] // 2
    fr, fi = spec[:, :half], spec[:, half:]
    gr, gi = gated_ref[:, :half], gated_ref[:, half:]
    product = jnp.concatenate([gr * fr - gi * fi, gr * fi + gi * fr], axis=1)
    causal = inverse(
        product, (third_high, third_low), (fourth_high, fourth_low), cos_ref, sin_ref
    )
    causal_ref[...] = causal
    mixed_ref[...] = (q_ref[...].astype(F32) * causal).astype(BF)


def grad_kernel(
    scale, b_ref, q_ref, k_ref, v_ref, causal_ref, filter_ref, gated_ref,
    first_high, first_low, second_high, second_low,
    third_high, third_low, fourth_high, fourth_low, cos_ref, sin_ref,
    gf_ref, act_ref, spec_ref,
):
    back = b_ref[...].astype(F32)
    high, low = split(back * q_ref[...].astype(F32))
    spec_ref[...] = forward(
        high, low, (first_high, first_low), (second_high, second_low), cos_ref, sin_ref
    )
    half = spec_ref.shape[1] // 2

    def correlate(other_ref):
        cr, ci = spec_ref[:, :half], spec_ref[:, half:]
        xr, xi = other_ref[:, :half], other_ref[:, half:]
        product = jnp.concatenate([xr * cr + xi * ci, xr * ci - xi * cr], axis=1)
        return inverse(
            product, (third_high, third_low), (fourth_high, fourth_low), cos_ref, sin_ref
        )

    gf_ref[...] = (correlate(gated_ref) * scale).astype(BF)
    gated_grad = correlate(filter_ref)
    act_ref[0] = (back * causal_ref[...]).astype(BF)
    act_ref[1] = (gated_grad * v_ref[...].astype(F32)).astype(BF)
    act_ref[2] = (gated_grad * k_ref[...].astype(F32)).astype(BF)


def rows_kernel(ids_ref, act_ref, out_ref, acc_ref):
    blocks, rows = ids_ref.shape
    vocab = out_ref.shape[0]
    chans = act_ref.shape[1] // blocks
    labels = lax.broadcasted_iota(jnp.int32, (vocab, rows), 0)
    acc_ref[...] = jnp.zeros_like(acc_ref)

    def body(s, carry):
        onehot = (labels == ids_ref[pl.ds(s, 1), :]).astype(F32).astype(BF)
        place = pl.ds(pl.multiple_of(s * chans, chans), chans)
        act = jnp.concatenate([act_ref[j, place, :] for j in range(3)], axis=0)
        acc_ref[...] += lax.dot_general(
            onehot, act, (((1,), (1,)), ((), ())), preferred_element_type=F32
        )
        return carry

    lax.fori_loop(0, blocks, body, 0)
    out_ref[...] = acc_ref[...].astype(BF)


PARAMS = pltpu.CompilerParams(vmem_limit_bytes=48 * 1024 * 1024)


def shards(token_ids, table, filter_raw, w_out, cotangent):
    rows = token_ids.shape[0]
    blocks = lax.axis_size("ctx")
    width = filter_raw.shape[1]
    chans = width // blocks
    vocab = table.shape[0]
    length = rows * blocks
    position = lax.axis_index("ctx")
    scale = 1.0 / math.sqrt(length)
    first, second, third, fourth, cosine, sine = tables(blocks, chans, rows)
    field = jax.ShapeDtypeStruct((blocks * chans, rows), BF)
    wide = jax.ShapeDtypeStruct((blocks * chans, 2 * rows), F32)
    forward_args = (*first, *second)
    inverse_args = (*third, *fourth)

    def exchange(values):
        return lax.all_to_all(values, "ctx", split_axis=0, concat_axis=0, tiled=True)

    ids = lax.all_gather(token_ids, "ctx", axis=0, tiled=False)
    filter_field = exchange(filter_raw.astype(BF).T)
    cot_full = lax.all_gather(cotangent, "tp", axis=1, tiled=True)

    local = lax.dynamic_slice(table, (0, 0, position * chans), (vocab, 3, chans))
    local = local.transpose(1, 2, 0).reshape(3 * chans, vocab)
    query, key, value = pl.pallas_call(
        embed_kernel, out_shape=(field, field, field), compiler_params=PARAMS, name="embed"
    )(ids, local)
    gated_spec = pl.pallas_call(
        input_kernel, out_shape=wide, compiler_params=PARAMS, name="gated_spectrum"
    )(key, value, *forward_args, cosine, sine)
    filter_spec, causal, mixed = pl.pallas_call(
        functools.partial(causal_kernel, scale),
        out_shape=(wide, jax.ShapeDtypeStruct(field.shape, F32), field),
        compiler_params=PARAMS,
        name="causal",
    )(filter_field, query, gated_spec, *forward_args, *inverse_args, cosine, sine)
    mixed_rows = exchange(mixed)
    partial_out = lax.dot_general(
        mixed_rows, w_out, (((0,), (0,)), ((), ())), preferred_element_type=F32
    )
    output = lax.psum_scatter(partial_out.astype(BF), "tp", scatter_dimension=1, tiled=True)

    back = lax.dot_general(
        w_out, cot_full, (((1,), (1,)), ((), ())), preferred_element_type=F32
    )
    back_field = exchange(back.astype(BF))
    filter_grad, act = pl.pallas_call(
        functools.partial(grad_kernel, scale),
        out_shape=(field, jax.ShapeDtypeStruct((3,) + field.shape, BF)),
        scratch_shapes=[pltpu.VMEM(wide.shape, F32)],
        compiler_params=PARAMS,
        name="grads",
    )(
        back_field, query, key, value, causal, filter_spec, gated_spec,
        *forward_args, *inverse_args, cosine, sine,
    )
    grad_filter = exchange(filter_grad).T.astype(F32)
    row_sums = pl.pallas_call(
        rows_kernel,
        out_shape=jax.ShapeDtypeStruct((vocab, 3 * chans), BF),
        scratch_shapes=[pltpu.VMEM((vocab, 3 * chans), F32)],
        compiler_params=PARAMS,
        name="row_sums",
    )(ids, act)
    grad_rows = exchange(row_sums)
    vocab_rows = vocab // blocks
    grad_rows = grad_rows.reshape(blocks, vocab_rows, 3, chans).transpose(1, 2, 0, 3)
    grad_table = grad_rows.reshape(vocab_rows, 3, width).astype(F32)
    return (output, grad_filter, grad_table)


def solution(mesh):
    return jax.shard_map(
        shards,
        mesh=mesh,
        in_specs=(P("ctx"), P(None, None, "tp"), P("ctx", "tp"), P("tp", None), P("ctx", "tp")),
        out_specs=(P("ctx", "tp"), P("ctx", "tp"), P("ctx", None, "tp")),
        check_vma=False,
    )
```

time: 538 us -> 155 us (0.29)
  the two profiles are of different devices: /device:TPU:6 before, /device:TPU:1 now
where the time goes in v1:
time: 155 us; the launch traced here: 154 us
  blocking collectives  61.4 us (40%)
  Pallas kernels  33.4 us (22%)
  local copies, waits for them, and re-layouts  17.1 us (11%)
  between operations  14.3 us (9%)
  starting transfers between devices  12.6 us (8%)
  waiting for transfers between devices  8 us (5%)
  matrix products  6.9 us (4%)
    all_to_all x3, blocking collectives, exchange(): lax.all_to_all(values, 'ctx', split_axis=0, concat_axis=0, tiled=True)  36.9 us
    all_gather x1, blocking collectives, shards(): ids = lax.all_gather(token_ids, 'ctx', axis=0, tiled=False)  24.5 us
    unnamed x59, local copies, waits for them, and re-layouts  15.2 us
    all_to_all x2, starting transfers between devices, exchange(): lax.all_to_all(values, 'ctx', split_axis=0, concat_axis=0, tiled=True)  12.6 us
    pallas_call x1, Pallas kernels, shards(): pl.pallas_call(functools.partial(grad_kernel, scale), out_shape=(field, j...  9.56 us
    pallas_call x1, Pallas kernels, shards(): pl.pallas_call(functools.partial(causal_kernel, scale), out_shape=(wide,...  8.43 us
    all_to_all x2, waiting for transfers between devices, exchange(): lax.all_to_all(values, 'ctx', split_axis=0, concat_axis=0, tiled=True)  7.28 us
    pallas_call x1, Pallas kernels, shards(): pl.pallas_call(rows_kernel, out_shape=jax.ShapeDtypeStruct((vocab, 3 * ch...  6.76 us
  transfers between devices with their start and end apart: 4, of which 1 were waited for; matrix products, arithmetic and copies ran while one was open for 8% of the time, Pallas kernels for 22%

profile of v1, /device:TPU:1, one launch (start us, length us, event | category | flops | bytes accessed | tf_op | source)
XLA Modules:
  0.0 153.9 jit_solution(4067064673419558032)
XLA Ops:
  8.0 1.9 %copy.27 = bf16[256,512]{0,1:T(8,128)(2,1)} copy(f32[256,512]{1,0:T(8,128)} %param.17) | data formatting | bytes 786432 | tf_op args[2]
  9.8 8.6 %all-to-all-start = ((bf16[32,16,256]{2,1,0:T(8,128)(2,1)}), bf16[32,16,256]{2,1,0:T(8,128)(2,1)}, u32[]{:S(2)}, u32[]{:S(2)}) async-start(bf16[32,16,256]{2,1,0:T(8,128)(2,1)} %bitcast.1), calls=%async_computation | async-start | bytes 524288 | tf_op jit(solution)/shard_map/all_to_all | solution.py:208
  18.5 24.5 %all-gather.1 = s32[32,1,256]{2,1,0:T(1,128)S(1)} all-gather(s32[1,1,256]{2,1,0:T(1,128)} %bitcast.44), channel_id=2, replica_groups=mesh['ctx'=32,'tp'=8] {'ctx'}, dimensions={0}, use_global_device_ids=true | all-gather | bytes 33792 | tf_op jit(solution)/shard_map/all_gather | solution.py:210
  43.4 5.3 %embed.1 = (bf16[512,256]{1,0:T(8,128)(2,1)S(1)}, bf16[512,256]{1,0:T(8,128)(2,1)S(1)}, bf16[512,256]{1,0:T(8,128)(2,1)S(1)}) custom-call(s32[32,256]{1,0:T(8,128)S(1)} %bitcast.36, bf16[48,512]{1,0:T(8,128)(2,1)S(1)} %bitcast.40), custom_call_target="tpu_custom_call" | custom-call | tf_op jit(solution)/shard_map/embed/pallas_call | solution.py:216
  48.7 1.2 copy-done.1
  49.9 1.2 copy-done.2
  51.1 1.0 copy-done.4
  52.2 1.0 copy-done.6
  54.7 3.4 %gated_spectrum.1.gated_ref = f32[512,512]{1,0:T(8,128)S(1)} custom-call(bf16[512,256]{1,0:T(8,128)(2,1)S(1)} %get-tuple-element.12.k_ref, bf16[512,256]{1,0:T(8,128)(2,1)S(1)} %get-tuple-element.13.v_ref, bf16[1024,512]{1,0:T(8,128)(2,1)S(1)} %copy-done.2, bf16[1024,512]{1,0:T(8,128)(2,1)S(1)} %copy-done.1, bf16[512,512]{1,0:T(8,128)(2,1)S(1)} %copy-done.6, ...), custom_call_target="tpu_custom_call" | custom-call | tf_op jit(solution)/shard_map/gated_spectrum/pallas_call | solution.py:219
  59.6 1.4 copy-done.7
  61.0 1.0 copy-done.9
  62.0 1.0 copy-done.11
  63.1 8.4 %causal.1 = (f32[512,512]{1,0:T(8,128)S(1)}, f32[512,256]{1,0:T(8,128)S(1)}, bf16[512,256]{1,0:T(8,128)(2,1)S(1)}) custom-call(bf16[512,256]{1,0:T(8,128)(2,1)} %bitcast.2.f_ref, bf16[512,256]{1,0:T(8,128)(2,1)S(1)} %get-tuple-element.11.q_ref, f32[512,512]{1,0:T(8,128)S(1)} %gated_spectrum.1.gated_ref, bf16[1024,512]{1,0:T(8,128)(2,1)} %constant.32.clone.first_high, ...), custom_call_target="tpu_custom_call" | custom-call | tf_op jit(solution)/shard_map/causal/pallas_call | solution.py:222
  72.5 13.6 %all_to_all.52 = bf16[32,16,256]{2,1,0:T(8,128)(2,1)S(1)} all-to-all(bf16[32,16,256]{2,1,0:T(8,128)(2,1)S(1)} %bitcast.39), channel_id=1, replica_groups=mesh['ctx'=32,'tp'=8] {'ctx'}, dimensions={0} | all-to-all | bytes 524288 | tf_op jit(solution)/shard_map/all_to_all | solution.py:208
  86.2 2.6 %convolution_convert_fusion = bf16[256,4096]{1,0:T(8,128)(2,1)} fusion(bf16[512,256]{1,0:T(8,128)(2,1)S(1)} %bitcast.41, bf16[512,4096]{1,0:T(8,128)(2,1)S(1)} %copy-done.26), kind=kOutput, calls=%fused_computation | convolution fusion | flops 1074790400 | bytes 6553600 | tf_op jit(solution)/shard_map/dot_general | solution.py:229
  88.9 4.3 %convolution_convert_fusion.1 = bf16[512,256]{1,0:T(8,128)(2,1)S(1)} fusion(bf16[512,4096]{1,0:T(8,128)(2,1)} %param.18, bf16[256,4096]{1,0:T(8,128)(2,1)} %all-gather.4.cloned.1.call-done), kind=kOutput, calls=%fused_computation.1 | convolution fusion | flops 1073872896 | bytes 6553600 | tf_op jit(solution)/shard_map/dot_general | solution.py:234
  93.2 12.5 %all_to_all.53 = bf16[32,16,256]{2,1,0:T(8,128)(2,1)S(1)} all-to-all(bf16[32,16,256]{2,1,0:T(8,128)(2,1)S(1)} %bitcast.43), channel_id=1, replica_groups=mesh['ctx'=32,'tp'=8] {'ctx'}, dimensions={0} | all-to-all | bytes 524288 | tf_op jit(solution)/shard_map/all_to_all | solution.py:208
  105.7 9.6 %grads.1 = (bf16[512,256]{1,0:T(8,128)(2,1)S(1)}, bf16[3,512,256]{2,1,0:T(8,128)(2,1)S(1)}) custom-call(bf16[512,256]{1,0:T(8,128)(2,1)S(1)} %bitcast.34, bf16[512,256]{1,0:T(8,128)(2,1)S(1)} %get-tuple-element.11.q_ref, bf16[512,256]{1,0:T(8,128)(2,1)S(1)} %copy-done.16, bf16[512,256]{1,0:T(8,128)(2,1)S(1)} %copy-done.18, f32[512,256]{1,0:T(8,128)S(1)} %copy-done.20, ...), custom_call_target="tpu_custom_call" | custom-call | tf_op jit(solution)/shard_map/grads/pallas_call | solution.py:238
  115.3 6.8 %row_sums.1 = bf16[512,48]{1,0:T(8,128)(2,1)S(1)} custom-call(s32[32,256]{1,0:T(8,128)S(1)} %bitcast.37, bf16[3,512,256]{2,1,0:T(8,128)(2,1)S(1)} %get-tuple-element.18.act_ref), custom_call_target="tpu_custom_call" | custom-call | tf_op jit(solution)/shard_map/row_sums/pallas_call | solution.py:249
  122.3 10.8 %all_to_all.54 = bf16[32,2,384]{2,1,0:T(2,128)(2,1)S(1)} all-to-all(bf16[32,2,384]{2,1,0:T(2,128)(2,1)S(1)} %reshape.36), channel_id=1, replica_groups=mesh['ctx'=32,'tp'=8] {'ctx'}, dimensions={0} | all-to-all | bytes 98304 | tf_op jit(solution)/shard_map/all_to_all | solution.py:208
  133.1 3.9 %all-to-all-start.3 = ((bf16[32,16,256]{2,1,0:T(8,128)(2,1)}), bf16[32,16,256]{2,1,0:T(8,128)(2,1)S(1)}, u32[]{:S(2)}, u32[]{:S(2)}) async-start(bf16[32,16,256]{2,1,0:T(8,128)(2,1)} %bitcast.38), calls=%async_computation.4 | async-start | bytes 524288 | tf_op jit(solution)/shard_map/all_to_all | solution.py:208
  137.7 1.0 reshape.29
  138.7 7.3 %all-to-all-done.3 = bf16[32,16,256]{2,1,0:T(8,128)(2,1)S(1)} async-done(((bf16[32,16,256]{2,1,0:T(8,128)(2,1)}), bf16[32,16,256]{2,1,0:T(8,128)(2,1)S(1)}, u32[]{:S(2)}, u32[]{:S(2)}) %all-to-all-start.3) | async-done | bytes 262176 | tf_op jit(solution)/shard_map/all_to_all | solution.py:208
  146.1 1.0 copy.31
  (63 shorter events, 6.1 us)
Async XLA Ops:
  7.2 35.9 %copy-start = (bf16[512,3,512]{2,0,1:T(8,128)(2,1)S(1)}, bf16[512,3,512]{2,0,1:T(8,128)(2,1)}, u32[]{:S(2)}) copy-start(bf16[512,3,512]{2,0,1:T(8,128)(2,1)} %param.16) | copy-start | bytes 4718596
  7.2 52.4 %copy-start.22 = (f32[32,256]{1,0:T(8,128)S(1)}, f32[32,256]{1,0:T(8,128)}, u32[]{:S(2)}) copy-start(f32[32,256]{1,0:T(8,128)} %constant.37.clone.sin_ref) | copy-start | bytes 98308
  7.2 52.4 %copy-start.24 = (f32[32,256]{1,0:T(8,128)S(1)}, f32[32,256]{1,0:T(8,128)}, u32[]{:S(2)}) copy-start(f32[32,256]{1,0:T(8,128)} %constant.36.clone.cos_ref) | copy-start | bytes 98308
  7.2 52.4 %copy-start.5 = (bf16[512,512]{1,0:T(8,128)(2,1)S(1)}, bf16[512,512]{1,0:T(8,128)(2,1)}, u32[]{:S(2)}) copy-start(bf16[512,512]{1,0:T(8,128)(2,1)} %constant.35.clone.second_low) | copy-start | bytes 1572868
  7.2 81.7 %all-gather.4.cloned.1.call-start = ((), (), s32[]{:S(2)}) async-start(), calls=%async_computation.7 | async-start | bytes 2359296 | tf_op jit(solution)/shard_map/all_gather | solution.py:212
  9.8 49.7 %all-to-all-start = ((bf16[32,16,256]{2,1,0:T(8,128)(2,1)}), bf16[32,16,256]{2,1,0:T(8,128)(2,1)}, u32[]{:S(2)}, u32[]{:S(2)}) async-start(bf16[32,16,256]{2,1,0:T(8,128)(2,1)} %bitcast.1), calls=%async_computation | async-start | bytes 524288 | tf_op jit(solution)/shard_map/all_to_all | solution.py:208
  18.5 128.6 %reduce-scatter.2.cloned.1.call-start = ((), (), s32[]{:S(2)}) async-start(), calls=%async_computation.6 | async-start | bytes 2359296 | tf_op jit(solution)/shard_map/reduce_scatter | solution.py:232
  48.7 1.2 copy-start.1
  49.9 1.2 copy-start.2
  51.1 1.0 copy-start.4
  52.2 1.0 copy-start.6
  59.6 26.6 %copy-start.3 = (f32[512,512]{1,0:T(8,128)}, f32[512,512]{1,0:T(8,128)S(1)}, u32[]{:S(2)}) copy-start(f32[512,512]{1,0:T(8,128)S(1)} %gated_spectrum.1.gated_ref) | copy-start | bytes 3145732
  59.6 1.4 copy-start.7
  63.1 23.1 %copy-start.26 = (bf16[512,4096]{1,0:T(8,128)(2,1)S(1)}, bf16[512,4096]{1,0:T(8,128)(2,1)}, u32[]{:S(2)}) copy-start(bf16[512,4096]{1,0:T(8,128)(2,1)} %param.18) | copy-start | bytes 12582916
  72.5 13.7 %copy-start.19 = (f32[512,256]{1,0:T(8,128)}, f32[512,256]{1,0:T(8,128)S(1)}, u32[]{:S(2)}) copy-start(f32[512,256]{1,0:T(8,128)S(1)} %get-tuple-element.15.causal_ref) | copy-start | bytes 1572868
  88.8 16.9 %copy-start.8 = (bf16[512,512]{1,0:T(8,128)(2,1)S(1)}, bf16[512,512]{1,0:T(8,128)(2,1)}, u32[]{:S(2)}) copy-start(bf16[512,512]{1,0:T(8,128)(2,1)} %constant.34.clone.second_high) | copy-start | bytes 1572868
  88.8 16.9 %copy-start.10 = (bf16[512,512]{1,0:T(8,128)(2,1)S(1)}, bf16[512,512]{1,0:T(8,128)(2,1)}, u32[]{:S(2)}) copy-start(bf16[512,512]{1,0:T(8,128)(2,1)} %constant.39.clone.third_low) | copy-start | bytes 1572868
  88.9 16.8 %copy-start.12 = (bf16[512,512]{1,0:T(8,128)(2,1)S(1)}, bf16[512,512]{1,0:T(8,128)(2,1)}, u32[]{:S(2)}) copy-start(bf16[512,512]{1,0:T(8,128)(2,1)} %constant.38.clone.third_high) | copy-start | bytes 1572868
  88.9 16.8 %copy-start.14 = (f32[512,512]{1,0:T(8,128)S(1)}, f32[512,512]{1,0:T(8,128)}, u32[]{:S(2)}) copy-start(f32[512,512]{1,0:T(8,128)} %copy-done.13) | copy-start | bytes 3145732
  88.9 16.8 %copy-start.16 = (bf16[512,256]{1,0:T(8,128)(2,1)S(1)}, bf16[512,256]{1,0:T(8,128)(2,1)}, u32[]{:S(2)}) copy-start(bf16[512,256]{1,0:T(8,128)(2,1)} %copy-done.15) | copy-start | bytes 786436
  88.9 16.8 %copy-start.18 = (bf16[512,256]{1,0:T(8,128)(2,1)S(1)}, bf16[512,256]{1,0:T(8,128)(2,1)}, u32[]{:S(2)}) copy-start(bf16[512,256]{1,0:T(8,128)(2,1)} %copy-done.17) | copy-start | bytes 786436
  88.9 16.8 %copy-start.20 = (f32[512,256]{1,0:T(8,128)S(1)}, f32[512,256]{1,0:T(8,128)}, u32[]{:S(2)}) copy-start(f32[512,256]{1,0:T(8,128)} %copy-done.19) | copy-start | bytes 1572868
  115.3 6.8 %copy-start.25 = (bf16[512,256]{1,0:T(8,128)(2,1)}, bf16[512,256]{1,0:T(8,128)(2,1)S(1)}, u32[]{:S(2)}) copy-start(bf16[512,256]{1,0:T(8,128)(2,1)S(1)} %get-tuple-element.17) | copy-start | bytes 786436
  133.1 12.9 %all-to-all-start.3 = ((bf16[32,16,256]{2,1,0:T(8,128)(2,1)}), bf16[32,16,256]{2,1,0:T(8,128)(2,1)S(1)}, u32[]{:S(2)}, u32[]{:S(2)}) async-start(bf16[32,16,256]{2,1,0:T(8,128)(2,1)} %bitcast.38), calls=%async_computation.4 | async-start | bytes 524288 | tf_op jit(solution)/shard_map/all_to_all | solution.py:208
  (7 other events, 6.0 us)
Sparse Core Ops, SparseCore 0:
  9.8 41.3 all-gather.3
  88.9 36.8 reduce-scatter.1

commit v2 on v1

v2 whole, which is shorter than its diff:
```python
import functools
import math

import jax
import jax.numpy as jnp
import ml_dtypes
import numpy as np
from jax import lax
from jax.experimental import pallas as pl
from jax.experimental.pallas import tpu as pltpu
from jax.sharding import PartitionSpec as P

BF = jnp.bfloat16
F32 = jnp.float32


def split_np(values):
    high = values.astype(np.float32).astype(ml_dtypes.bfloat16)
    low = (values - high.astype(np.float64)).astype(np.float32).astype(ml_dtypes.bfloat16)
    return high, low


@functools.lru_cache(maxsize=None)
def tables(blocks, chans, rows):
    period = 2 * blocks * rows
    s = np.arange(blocks, dtype=np.float64)
    r = np.arange(rows, dtype=np.float64)
    odd = np.arange(blocks, dtype=np.float64) + 0.5
    outer = 2 * np.pi * odd[:, None] * s[None, :] / (2 * blocks)
    eye = np.eye(chans)
    real = np.einsum("ks,cd->cksd", np.cos(outer), eye).reshape(chans * blocks, blocks * chans)
    imag = np.einsum("ks,cd->cksd", -np.sin(outer), eye).reshape(chans * blocks, blocks * chans)
    first = np.concatenate([real, imag], axis=0)
    inner = 2 * np.pi * (np.outer(r, r) % rows) / rows
    cosine, sine = np.cos(inner), np.sin(inner)
    second = np.block([[cosine, -sine], [sine, cosine]])
    twist = 2 * np.pi * odd[:, None] * r[None, :] / period
    return (
        *split_np(first),
        *split_np(second),
        *split_np(second.T.copy()),
        *split_np(first.T * (2.0 / period)),
        np.cos(twist).astype(np.float32),
        np.sin(twist).astype(np.float32),
    )


def split(values):
    high = values.astype(BF)
    return high, (values - high.astype(F32)).astype(BF)


def mm(left, right):
    return jnp.dot(left, right, preferred_element_type=F32)


def twiddle(real, imag, cos_ref, sin_ref, sign):
    rows, lanes = real.shape
    blocks = cos_ref.shape[0]
    shape = (rows // blocks, blocks, lanes)
    cosine = cos_ref[...][None]
    sine = sin_ref[...][None] * sign
    real = real.reshape(shape)
    imag = imag.reshape(shape)
    return (
        (real * cosine + imag * sine).reshape(rows, lanes),
        (imag * cosine - real * sine).reshape(rows, lanes),
    )


def forward(values, low_too, constants):
    first_high, first_low, second_high, second_low = constants[:4]
    cos_ref, sin_ref = constants[8:]
    high, low = split(values)
    stage = mm(first_high[...], high) + mm(first_low[...], high)
    if low_too:
        stage = stage + mm(first_high[...], low)
    half = stage.shape[0] // 2
    real, imag = twiddle(stage[:half], stage[half:], cos_ref, sin_ref, 1.0)
    high, low = split(jnp.concatenate([real, imag], axis=1))
    return mm(high, second_high[...]) + mm(low, second_high[...]) + mm(high, second_low[...])


def inverse(real, imag, constants):
    third_high, third_low, fourth_high, fourth_low, cos_ref, sin_ref = constants[4:]
    high, low = split(jnp.concatenate([real, imag], axis=1))
    stage = mm(high, third_high[...]) + mm(low, third_high[...]) + mm(high, third_low[...])
    half = stage.shape[1] // 2
    real, imag = twiddle(stage[:, :half], stage[:, half:], cos_ref, sin_ref, -1.0)
    high, low = split(jnp.concatenate([real, imag], axis=0))
    return mm(fourth_high[...], high) + mm(fourth_high[...], low) + mm(fourth_low[...], high)


def spread(values, wide_ref):
    wide_ref[...] = values.reshape(wide_ref.shape)


def group_of(wide_ref, group):
    blocks, _, size, lanes = wide_ref.shape
    return wide_ref[:, group].reshape(blocks * size, lanes)


def joined(wide_ref):
    blocks, groups, size, lanes = wide_ref.shape
    return wide_ref[...].reshape(blocks * groups * size, lanes)


def fetch(sources, targets, sems):
    copies = [
        pltpu.make_async_copy(source, target, sems.at[place])
        for place, (source, target) in enumerate(zip(sources, targets))
    ]
    for copy in copies:
        copy.start()
    return copies


def wait_all(copies):
    for copy in copies:
        copy.wait()


def onehots(ids_ref, s, chans, vocab):
    quarter = chans // 4
    lanes = ids_ref.shape[1]
    block = ids_ref[pl.ds(pl.multiple_of(s * chans, chans), chans), :]
    block = block.astype(F32)
    labels = lax.broadcasted_iota(jnp.int32, (16, lanes), 0).astype(F32)
    halves = []
    for half in range(2):
        coarse = jnp.broadcast_to(block[half * quarter : half * quarter + 1], (16, lanes))
        fine = block[(2 + half) * quarter : (2 + half) * quarter + 1]
        fine_hot = (labels == fine).astype(F32).astype(BF)
        coarse = coarse.astype(BF)
        zero = jnp.zeros_like(fine_hot)
        halves.append(
            jnp.concatenate(
                [
                    jnp.where(coarse == jnp.array(part, BF), fine_hot, zero)
                    for part in range(vocab // 16)
                ],
                axis=0,
            )
        )
    return jnp.concatenate(halves, axis=1)


def send_kernel(f_ref, ids_ref, out_ref):
    rows, width = f_ref.shape
    out_ref[:, :rows] = f_ref[...].T.astype(BF)
    ids = ids_ref[...]
    coarse = ids // 16
    pieces = (coarse, ids - 16 * coarse)
    lanes = 128
    quarters = [
        jnp.broadcast_to(piece[:, half * lanes : (half + 1) * lanes].astype(F32), (4, lanes))
        for piece in pieces
        for half in range(2)
    ]
    tile = jnp.concatenate(quarters, axis=0).astype(BF)
    for start in range(0, width, 16):
        out_ref[start : start + 16, rows:] = tile


def front_kernel(
    scale, in_ref, tab_ref, *refs,
):
    constants_hbm, refs = refs[:10], refs[10:]
    outs, refs = refs[:7], refs[7:]
    mixed_ref, refs = refs[0], refs[1:]
    constants, refs = refs[:10], refs[10:]
    held, refs = refs[:7], refs[7:]
    wide_ref, in_sems, out_sems = refs
    q_ref, k_ref, v_ref, ids_ref, filter_ref, gated_ref, causal_ref = held
    incoming = fetch(constants_hbm, constants, in_sems)
    rows = q_ref.shape[1]
    chans = tab_ref.shape[0] // 3
    vocab = tab_ref.shape[1]
    blocks = q_ref.shape[0] // chans
    part = q_ref.shape[0] // 2

    def leave(first, last):
        copies = [
            pltpu.make_async_copy(held[place], outs[place], out_sems.at[place])
            for place in range(first, last)
        ]
        for copy in copies:
            copy.start()
        return copies

    ids_ref[...] = in_ref[:, rows:]

    def body(s, carry):
        picked = mm(tab_ref[...], onehots(ids_ref, s, chans, vocab)).astype(BF)
        place = pl.ds(pl.multiple_of(s * chans, chans), chans)
        q_ref[place, :] = picked[:chans]
        k_ref[place, :] = picked[chans : 2 * chans]
        v_ref[place, :] = picked[2 * chans :]
        return carry

    lax.fori_loop(0, blocks, body, 0, unroll=2)
    leaving = leave(0, 4)
    wait_all(incoming)
    spread(in_ref[:, :rows].astype(F32), wide_ref)
    for group in range(2):
        place = slice(group * part, (group + 1) * part)
        filter_ref[place] = forward(group_of(wide_ref, group), False, constants) * scale
    leaving += leave(4, 5)
    spread(k_ref[...].astype(F32) * v_ref[...].astype(F32), wide_ref)
    for group in range(2):
        place = slice(group * part, (group + 1) * part)
        gated_ref[place] = forward(group_of(wide_ref, group), True, constants)
    leaving += leave(5, 6)
    size = wide_ref.shape[2]
    for group in range(2):
        place = slice(group * part, (group + 1) * part)
        fr, fi = filter_ref[place, :rows], filter_ref[place, rows:]
        gr, gi = gated_ref[place, :rows], gated_ref[place, rows:]
        causal = inverse(gr * fr - gi * fi, gr * fi + gi * fr, constants)
        wide_ref[:, group] = causal.reshape(blocks, size, rows)
    causal = joined(wide_ref)
    causal_ref[...] = causal
    leaving += leave(6, 7)
    mixed_ref[...] = (q_ref[...].astype(F32) * causal).astype(BF)
    wait_all(leaving)


def back_kernel(scale, b_ref, *refs):
    sources, refs = refs[:17], refs[17:]
    out_ref, refs = refs[0], refs[1:]
    held, refs = refs[:17], refs[17:]
    act_ref, spec_ref, acc_ref, wide_ref, sems = refs
    incoming = fetch(sources, held, sems)
    constants, q_ref, causal_ref, gated_ref, filter_ref, k_ref, v_ref, ids_ref = (
        (*held[1:5], *held[8:12], *held[5:7]), held[0], held[12], held[7], *held[13:]
    )
    rows = b_ref.shape[1]
    blocks = act_ref.shape[0]
    chans = b_ref.shape[0] // blocks
    vocab = acc_ref.shape[0]
    part = b_ref.shape[0] // 2
    size = wide_ref.shape[2]
    shape = (blocks, chans, rows)
    wait_all(incoming[:7])
    spread(b_ref[...].astype(F32) * q_ref[...].astype(F32), wide_ref)
    for group in range(2):
        place = slice(group * part, (group + 1) * part)
        spec_ref[place] = forward(group_of(wide_ref, group), True, constants)

    def correlate(other_ref):
        for group in range(2):
            place = slice(group * part, (group + 1) * part)
            cr, ci = spec_ref[place, :rows], spec_ref[place, rows:]
            xr, xi = other_ref[place, :rows], other_ref[place, rows:]
            result = inverse(xr * cr + xi * ci, xr * ci - xi * cr, constants)
            wide_ref[:, group] = result.reshape(blocks, size, rows)
        return joined(wide_ref)

    wait_all(incoming[7:])
    out_ref[:, :rows] = (correlate(gated_ref) * scale).astype(BF)
    act_ref[:, :chans] = (b_ref[...].astype(F32) * causal_ref[...]).astype(BF).reshape(shape)
    gated_grad = correlate(filter_ref)
    act_ref[:, chans : 2 * chans] = (
        (gated_grad * v_ref[...].astype(F32)).astype(BF).reshape(shape)
    )
    act_ref[:, 2 * chans : 3 * chans] = (
        (gated_grad * k_ref[...].astype(F32)).astype(BF).reshape(shape)
    )
    act_ref[:, 3 * chans :] = jnp.zeros((blocks, 128 - 3 * chans, rows), BF)
    acc_ref[...] = jnp.zeros_like(acc_ref)
    group = 4

    def body(step, carry):
        hot = jnp.concatenate(
            [onehots(ids_ref, step * group + g, chans, vocab) for g in range(group)], axis=1
        )
        act = jnp.concatenate([act_ref[step * group + g] for g in range(group)], axis=1)
        acc_ref[...] += lax.dot_general(
            hot, act, (((1,), (1,)), ((), ())), preferred_element_type=F32
        )
        return carry

    lax.fori_loop(0, blocks // group, body, 0)
    out_ref[:, rows:] = acc_ref[...].astype(BF)


def finish_kernel(in_ref, grad_ref, table_ref):
    width, rows = grad_ref.shape[1], grad_ref.shape[0]
    vocab_rows = table_ref.shape[1]
    chans = vocab_rows * width // in_ref.shape[0]
    grad_ref[...] = in_ref[:, :rows].astype(F32).T
    sums = in_ref[:, rows:]
    lanes = sums.shape[1]
    column = lax.broadcasted_iota(jnp.int32, (lanes, width), 1)
    row = lax.broadcasted_iota(jnp.int32, (lanes, width), 0)
    source = lax.broadcasted_iota(jnp.int32, (width, width), 0) // vocab_rows
    mine = source == lax.broadcasted_iota(jnp.int32, (width, width), 1) // chans
    pick = lax.broadcasted_iota(jnp.int32, (vocab_rows, width), 1) % vocab_rows
    pick = pick == lax.broadcasted_iota(jnp.int32, (vocab_rows, width), 0)
    pick = pick.astype(F32).astype(BF)
    for field in range(3):
        take = (row == field * chans + column % chans).astype(F32).astype(BF)
        spreaded = jnp.where(mine, mm(sums, take), 0.0).astype(BF)
        table_ref[field] = mm(pick, spreaded)


def params(mebibytes):
    return pltpu.CompilerParams(vmem_limit_bytes=mebibytes * 1024 * 1024)


HBM = pl.BlockSpec(memory_space=pltpu.HBM)
VMEM = pl.BlockSpec(memory_space=pltpu.VMEM)


def scratch(arrays):
    return [pltpu.VMEM(array.shape, array.dtype) for array in arrays]


def shards(token_ids, table, filter_raw, w_out, cotangent):
    rows = token_ids.shape[0]
    blocks = lax.axis_size("ctx")
    width = filter_raw.shape[1]
    chans = width // blocks
    vocab = table.shape[0]
    length = rows * blocks
    position = lax.axis_index("ctx")
    scale = 1.0 / math.sqrt(length)
    constants = tables(blocks, chans // 2, rows)
    struct = jax.ShapeDtypeStruct
    field = struct((width, rows), BF)
    spectrum = struct((width, 2 * rows), F32)
    parcel = struct((width, rows + 128), BF)
    kept = (field, field, field, struct((width, 128), BF), spectrum, spectrum, struct(field.shape, F32))
    spread_shape = pltpu.VMEM((blocks, 2, chans // 2, rows), F32)

    def exchange(values):
        return lax.all_to_all(values, "ctx", split_axis=0, concat_axis=0, tiled=True)

    sent = pl.pallas_call(
        send_kernel, out_shape=parcel, compiler_params=params(62), name="send"
    )(filter_raw, token_ids[None])
    received = exchange(sent)
    cot_full = lax.all_gather(cotangent, "tp", axis=1, tiled=True)

    local = lax.dynamic_slice(table, (0, 0, position * chans), (vocab, 3, chans))
    local = local.transpose(1, 2, 0).reshape(3 * chans, vocab)
    query, key, value, ids, filter_spec, gated_spec, causal, mixed = pl.pallas_call(
        functools.partial(front_kernel, scale),
        out_shape=(*kept, field),
        in_specs=[VMEM, VMEM] + [HBM] * 10,
        out_specs=(HBM,) * 7 + (VMEM,),
        scratch_shapes=[
            *scratch(constants),
            *scratch(kept),
            spread_shape,
            pltpu.SemaphoreType.DMA((10,)),
            pltpu.SemaphoreType.DMA((7,)),
        ],
        compiler_params=params(62),
        name="front",
    )(received, local, *constants)
    mixed_rows = exchange(mixed)
    partial_out = lax.dot_general(
        mixed_rows, w_out, (((0,), (0,)), ((), ())), preferred_element_type=F32
    )
    output = lax.psum_scatter(partial_out.astype(BF), "tp", scatter_dimension=1, tiled=True)

    back = lax.dot_general(
        w_out, cot_full, (((1,), (1,)), ((), ())), preferred_element_type=F32
    )
    back_field = exchange(back.astype(BF))
    operands = (
        query, *constants[:4], *constants[8:], gated_spec, *constants[4:8], causal,
        filter_spec, key, value, ids,
    )
    grads = pl.pallas_call(
        functools.partial(back_kernel, scale),
        out_shape=parcel,
        in_specs=[VMEM] + [HBM] * 17,
        scratch_shapes=[
            *scratch(operands),
            pltpu.VMEM((blocks, 128, rows), BF),
            pltpu.VMEM(spectrum.shape, F32),
            pltpu.VMEM((vocab, 128), F32),
            spread_shape,
            pltpu.SemaphoreType.DMA((17,)),
        ],
        compiler_params=params(62),
        name="back",
    )(back_field, *operands)
    grads = exchange(grads)
    vocab_rows = vocab // blocks
    grad_filter, grad_table = pl.pallas_call(
        finish_kernel,
        out_shape=(struct((rows, width), F32), struct((3, vocab_rows, width), F32)),
        compiler_params=params(8),
        name="finish",
    )(grads)
    return (output, grad_filter, grad_table.transpose(1, 0, 2))


def solution(mesh):
    return jax.shard_map(
        shards,
        mesh=mesh,
        in_specs=(P("ctx"), P(None, None, "tp"), P("ctx", "tp"), P("tp", None), P("ctx", "tp")),
        out_specs=(P("ctx", "tp"), P("ctx", "tp"), P("ctx", None, "tp")),
        check_vma=False,
    )
```

time: 155 us -> 111 us (0.72)
  blocking collectives: 61.4 us -> 39.8 us
  local copies, waits for them, and re-layouts: 17.1 us -> 1.69 us
  Pallas kernels: 33.4 us -> 27.1 us
  starting transfers between devices: 12.6 us -> 8.67 us
  matrix products: 6.9 us -> 8.96 us
  waiting for transfers between devices: 8 us -> 9.88 us
    all_gather x1 -> x0, blocking collectives: 24.5 us -> none  [shards(): ids = lax.all_gather(token_ids, 'ctx', axis=0, tiled=False)]
    unnamed x59 -> x4, local copies, waits for them, and re-layouts: 15.2 us -> 0.74 us
    pallas_call x5 -> x4, Pallas kernels: 33.4 us -> 27.1 us  [the longest x1 12.3 us: shards(): pl.pallas_call(functools.partial(back_kernel, scale), out_shape=parcel, i...]
    all_to_all x2 -> x1, starting transfers between devices: 12.6 us -> 8.59 us  [exchange(): lax.all_to_all(values, 'ctx', split_axis=0, concat_axis=0, tiled=True)]
    all_to_all x3, blocking collectives: 36.9 us -> 39.8 us  [exchange(): lax.all_to_all(values, 'ctx', split_axis=0, concat_axis=0, tiled=True)]
    dot_general x1, matrix products: 2.62 us -> 4.81 us  [shards(): lax.dot_general(mixed_rows, w_out, (((0,), (0,)), ((), ())), preferred_el...]
    all_to_all x2 -> x1, waiting for transfers between devices: 7.28 us -> 9.16 us  [exchange(): lax.all_to_all(values, 'ctx', split_axis=0, concat_axis=0, tiled=True)]
  transfers between devices with their start and end apart: 4 -> 3, of which waited for: 1 -> 1; matrix products, arithmetic and copies ran while one was open for 8% -> 9% of each run, Pallas kernels for 22% -> 23%
where the time goes in v2:
time: 111 us; the launch traced here: 110 us
  blocking collectives  39.8 us (36%)
  Pallas kernels  27.1 us (24%)
  between operations  14.1 us (13%)
  waiting for transfers between devices  9.88 us (9%)
  matrix products  8.96 us (8%)
  starting transfers between devices  8.67 us (8%)
  local copies, waits for them, and re-layouts  1.69 us (2%)
    all_to_all x3, blocking collectives, exchange(): lax.all_to_all(values, 'ctx', split_axis=0, concat_axis=0, tiled=True)  39.8 us
    pallas_call x1, Pallas kernels, shards(): pl.pallas_call(functools.partial(back_kernel, scale), out_shape=parcel, i...  12.3 us
    pallas_call x1, Pallas kernels, shards(): pl.pallas_call(functools.partial(front_kernel, scale), out_shape=(*kept,...  11.2 us
    all_to_all x1, waiting for transfers between devices, exchange(): lax.all_to_all(values, 'ctx', split_axis=0, concat_axis=0, tiled=True)  9.16 us
    all_to_all x1, starting transfers between devices, exchange(): lax.all_to_all(values, 'ctx', split_axis=0, concat_axis=0, tiled=True)  8.59 us
    dot_general x1, matrix products, shards(): lax.dot_general(mixed_rows, w_out, (((0,), (0,)), ((), ())), preferred_el...  4.81 us
    dot_general x1, matrix products, shards(): lax.dot_general(w_out, cot_full, (((1,), (1,)), ((), ())), preferred_elem...  4.15 us
  transfers between devices with their start and end apart: 3, of which 1 were waited for; matrix products, arithmetic and copies ran while one was open for 9% of the time, Pallas kernels for 23%

profile of v2, /device:TPU:1, one launch (start us, length us, event | category | flops | bytes accessed | tf_op | source)
XLA Modules:
  0.0 110.2 jit_solution(5829185027298646803)
XLA Ops:
  7.2 0.0 copy-start
  7.2 0.0 all-gather.2.cloned.1.call-start
  7.2 0.7 all-gather.2.cloned.1.call-update
  7.9 1.9 %send.1 = bf16[512,384]{1,0:T(8,128)(2,1)} custom-call(f32[256,512]{1,0:T(8,128)} %f_ref.1, s32[1,256]{1,0:T(1,128)} %bitcast.26), custom_call_target="tpu_custom_call" | custom-call | tf_op jit(solution)/shard_map/send/pallas_call | solution.py:339
  9.8 8.6 %all-to-all-start = ((bf16[32,16,384]{2,1,0:T(8,128)(2,1)}), bf16[32,16,384]{2,1,0:T(8,128)(2,1)S(1)}, u32[]{:S(2)}, u32[]{:S(2)}) async-start(bf16[32,16,384]{2,1,0:T(8,128)(2,1)} %bitcast.20), calls=%async_computation | async-start | bytes 786432 | tf_op jit(solution)/shard_map/all_to_all | solution.py:337
  18.4 0.0 reduce-scatter.2.cloned.1.call-start
  18.5 0.0 copy-done
  18.5 0.2 dynamic-slice_bitcast_fusion
  18.7 0.8 copy.18
  19.5 9.2 %all-to-all-done = bf16[32,16,384]{2,1,0:T(8,128)(2,1)S(1)} async-done(((bf16[32,16,384]{2,1,0:T(8,128)(2,1)}), bf16[32,16,384]{2,1,0:T(8,128)(2,1)S(1)}, u32[]{:S(2)}, u32[]{:S(2)}) %all-to-all-start) | async-done | bytes 393248 | tf_op jit(solution)/shard_map/all_to_all | solution.py:337
  28.6 0.0 copy-start.1
  28.6 0.7 copy-done.1
  29.3 11.2 %front.1 = (bf16[512,256]{1,0:T(8,128)(2,1)}, bf16[512,256]{1,0:T(8,128)(2,1)}, bf16[512,256]{1,0:T(8,128)(2,1)}, bf16[512,128]{1,0:T(8,128)(2,1)}, f32[512,512]...) custom-call(bf16[512,384]{1,0:T(8,128)(2,1)} %bitcast.19, ...), custom_call_target="tpu_custom_call" | custom-call | tf_op jit(solution)/shard_map/front/pallas_call | solution.py:347
  40.6 12.9 %all_to_all.45 = bf16[32,16,256]{2,1,0:T(8,128)(2,1)S(1)} all-to-all(bf16[32,16,256]{2,1,0:T(8,128)(2,1)} %bitcast.23), channel_id=1, replica_groups=mesh['ctx'=32,'tp'=8] {'ctx'}, dimensions={0} | all-to-all | bytes 524288 | tf_op jit(solution)/shard_map/all_to_all | solution.py:337
  53.5 4.8 %convolution_convert_fusion = bf16[256,4096]{1,0:T(8,128)(2,1)} fusion(bf16[512,256]{1,0:T(8,128)(2,1)S(1)} %bitcast.22, bf16[512,4096]{1,0:T(8,128)(2,1)} %param.18), kind=kOutput, calls=%fused_computation | convolution fusion | flops 1074790400 | bytes 6553600 | tf_op jit(solution)/shard_map/dot_general | solution.py:363
  58.3 0.0 reduce-scatter.2.cloned.1.call-update
  58.3 0.0 all-gather.2.cloned.1.call-done
  58.3 4.1 %convolution_convert_fusion.1 = bf16[512,256]{1,0:T(8,128)(2,1)S(1)} fusion(bf16[512,4096]{1,0:T(8,128)(2,1)} %param.18, bf16[256,4096]{1,0:T(8,128)(2,1)} %all-gather.2.cloned.1.call-done), kind=kOutput, calls=%fused_computation.1 | convolution fusion | flops 1073872896 | bytes 6553600 | tf_op jit(solution)/shard_map/dot_general | solution.py:368
  62.5 12.8 %all_to_all.46 = bf16[32,16,256]{2,1,0:T(8,128)(2,1)} all-to-all(bf16[32,16,256]{2,1,0:T(8,128)(2,1)S(1)} %bitcast.24), channel_id=1, replica_groups=mesh['ctx'=32,'tp'=8] {'ctx'}, dimensions={0} | all-to-all | bytes 524288 | tf_op jit(solution)/shard_map/all_to_all | solution.py:337
  75.3 12.3 %back.1 = bf16[512,384]{1,0:T(8,128)(2,1)} custom-call(bf16[512,256]{1,0:T(8,128)(2,1)} %bitcast.21, bf16[512,256]{1,0:T(8,128)(2,1)} %get-tuple-element.14.refs_0_, bf16[512,256]{1,0:T(8,128)(2,1)} %constant.32.clone.refs_0_.refs_1_, bf16[512,256]{1,0:T(8,128)(2,1)} %constant.33.clone.refs_1_.refs_2_, bf16[512,512]{1,0:T(8,128)(2,1)} %constant.34.clone.refs_2_.refs_3_, ...), custom_call_target="tpu_custom_call" | custom-call | tf_op jit(solution)/shard_map/back/pallas_call | solution.py:376
  87.6 14.1 %all_to_all.47 = bf16[32,16,384]{2,1,0:T(8,128)(2,1)S(1)} all-to-all(bf16[32,16,384]{2,1,0:T(8,128)(2,1)} %bitcast.18), channel_id=1, replica_groups=mesh['ctx'=32,'tp'=8] {'ctx'}, dimensions={0} | all-to-all | bytes 786432 | tf_op jit(solution)/shard_map/all_to_all | solution.py:337
  101.7 1.7 %finish.1 = (f32[256,512]{1,0:T(8,128)}, f32[3,16,512]{2,1,0:T(8,128)}) custom-call(bf16[512,384]{1,0:T(8,128)(2,1)S(1)} %bitcast.17), custom_call_target="tpu_custom_call" | custom-call | tf_op jit(solution)/shard_map/finish/pallas_call | solution.py:393
  103.4 0.0 reduce-scatter.2.cloned.1.call-done
Async XLA Ops:
  7.2 11.3 %copy-start = (bf16[512,3,512]{2,0,1:T(8,128)(2,1)S(1)}, bf16[512,3,512]{2,0,1:T(8,128)(2,1)}, u32[]{:S(2)}) copy-start(bf16[512,3,512]{2,0,1:T(8,128)(2,1)} %param.16) | copy-start | bytes 4718596
  7.2 51.2 %all-gather.2.cloned.1.call-start = ((), (), s32[]{:S(2)}) async-start(), calls=%async_computation.6 | async-start | bytes 2359296 | tf_op jit(solution)/shard_map/all_gather | solution.py:343
  9.8 18.8 %all-to-all-start = ((bf16[32,16,384]{2,1,0:T(8,128)(2,1)}), bf16[32,16,384]{2,1,0:T(8,128)(2,1)S(1)}, u32[]{:S(2)}, u32[]{:S(2)}) async-start(bf16[32,16,384]{2,1,0:T(8,128)(2,1)} %bitcast.20), calls=%async_computation | async-start | bytes 786432 | tf_op jit(solution)/shard_map/all_to_all | solution.py:337
  18.4 84.9 %reduce-scatter.2.cloned.1.call-start = ((), (), s32[]{:S(2)}) async-start(), calls=%async_computation.5 | async-start | bytes 2359296 | tf_op jit(solution)/shard_map/reduce_scatter | solution.py:366
  28.6 0.7 copy-start.1
Sparse Core Ops, SparseCore 0:
  9.8 41.3 all-gather.1
  58.4 36.8 reduce-scatter.1

commit v3 on v2

v3 whole, which is shorter than its diff:
```python
import functools
import math

import jax
import jax.numpy as jnp
import ml_dtypes
import numpy as np
from jax import lax
from jax.experimental import pallas as pl
from jax.experimental.pallas import tpu as pltpu
from jax.sharding import PartitionSpec as P

BF = jnp.bfloat16
F32 = jnp.float32


def split_np(values):
    high = values.astype(np.float32).astype(ml_dtypes.bfloat16)
    low = (values - high.astype(np.float64)).astype(np.float32).astype(ml_dtypes.bfloat16)
    return high, low


@functools.lru_cache(maxsize=None)
def tables(blocks, chans, rows):
    period = 2 * blocks * rows
    s = np.arange(blocks, dtype=np.float64)
    r = np.arange(rows, dtype=np.float64)
    odd = np.arange(blocks, dtype=np.float64) + 0.5
    outer = 2 * np.pi * odd[:, None] * s[None, :] / (2 * blocks)
    eye = np.eye(chans)
    real = np.einsum("ks,cd->cksd", np.cos(outer), eye).reshape(chans * blocks, blocks * chans)
    imag = np.einsum("ks,cd->cksd", -np.sin(outer), eye).reshape(chans * blocks, blocks * chans)
    first = np.concatenate([real, imag], axis=0)
    inner = 2 * np.pi * (np.outer(r, r) % rows) / rows
    cosine, sine = np.cos(inner), np.sin(inner)
    second = np.block([[cosine, -sine], [sine, cosine]])
    twist = 2 * np.pi * odd[:, None] * r[None, :] / period
    return np.concatenate(
        [
            np.concatenate(split_np(np.cos(twist)), axis=1),
            np.concatenate(split_np(np.sin(twist)), axis=1),
            np.concatenate(split_np(first), axis=1),
            *split_np(second),
            *split_np(second.T.copy()),
            *split_np(first.T * (2.0 / period)),
        ],
        axis=0,
    )


class Constants:
    def __init__(self, ref, blocks, rows):
        inner = ref.shape[1]
        start = 0

        def take(count):
            nonlocal start
            start += count
            return slice(start - count, start)

        cosine, sine, first = take(blocks), take(blocks), take(2 * rows)
        high, low = slice(0, rows), slice(rows, 2 * rows)
        self.cosine = lambda: ref[cosine, high].astype(F32) + ref[cosine, low].astype(F32)
        self.sine = lambda: ref[sine, high].astype(F32) + ref[sine, low].astype(F32)
        self.first = (ref.at[first, high], ref.at[first, low])
        self.second = (ref.at[take(inner)], ref.at[take(inner)])
        self.early = start
        self.third = (ref.at[take(inner)], ref.at[take(inner)])
        self.fourth = (ref.at[take(rows)], ref.at[take(rows)])


def split(values):
    high = values.astype(BF)
    return high, (values - high.astype(F32)).astype(BF)


def mm(left, right):
    return jnp.dot(left, right, preferred_element_type=F32)


def twiddle(real, imag, cosine, sine):
    rows, lanes = real.shape
    blocks = cosine.shape[0]
    shape = (rows // blocks, blocks, lanes)
    cosine = cosine[None]
    sine = sine[None]
    real = real.reshape(shape)
    imag = imag.reshape(shape)
    return (
        (real * cosine + imag * sine).reshape(rows, lanes),
        (imag * cosine - real * sine).reshape(rows, lanes),
    )


def forward(values, low_too, constants):
    first_high, first_low = constants.first
    second_high, second_low = constants.second
    high, low = split(values)
    stage = mm(first_high[...], high) + mm(first_low[...], high)
    if low_too:
        stage = stage + mm(first_high[...], low)
    half = stage.shape[0] // 2
    real, imag = twiddle(stage[:half], stage[half:], constants.cosine(), constants.sine())
    high, low = split(jnp.concatenate([real, imag], axis=1))
    return mm(high, second_high[...]) + mm(low, second_high[...]) + mm(high, second_low[...])


def inverse(real, imag, constants):
    third_high, third_low = constants.third
    fourth_high, fourth_low = constants.fourth
    high, low = split(jnp.concatenate([real, imag], axis=1))
    stage = mm(high, third_high[...]) + mm(low, third_high[...]) + mm(high, third_low[...])
    half = stage.shape[1] // 2
    real, imag = twiddle(stage[:, :half], stage[:, half:], constants.cosine(), -constants.sine())
    high, low = split(jnp.concatenate([real, imag], axis=0))
    return mm(fourth_high[...], high) + mm(fourth_high[...], low) + mm(fourth_low[...], high)


def spread(values, wide_ref):
    wide_ref[...] = values.reshape(wide_ref.shape)


def group_of(wide_ref, group):
    blocks, _, size, lanes = wide_ref.shape
    return wide_ref[:, group].reshape(blocks * size, lanes)


def joined(wide_ref):
    blocks, groups, size, lanes = wide_ref.shape
    return wide_ref[...].reshape(blocks * groups * size, lanes)


def started(copies):
    for copy in copies:
        copy.start()
    return copies


def onehots(ids_ref, s, chans, vocab):
    quarter = chans // 4
    lanes = ids_ref.shape[1]
    block = ids_ref[pl.ds(pl.multiple_of(s * chans, chans), chans), :]
    block = block.astype(F32)
    labels = lax.broadcasted_iota(jnp.int32, (16, lanes), 0).astype(F32)
    halves = []
    for half in range(2):
        coarse = jnp.broadcast_to(block[half * quarter : half * quarter + 1], (16, lanes))
        fine = block[(2 + half) * quarter : (2 + half) * quarter + 1]
        fine_hot = (labels == fine).astype(F32).astype(BF)
        coarse = coarse.astype(BF)
        zero = jnp.zeros_like(fine_hot)
        halves.append(
            jnp.concatenate(
                [
                    jnp.where(coarse == jnp.array(part, BF), fine_hot, zero)
                    for part in range(vocab // 16)
                ],
                axis=0,
            )
        )
    return jnp.concatenate(halves, axis=1)


def send_kernel(f_ref, ids_ref, out_ref):
    rows, width = f_ref.shape
    out_ref[:, :rows] = f_ref[...].T.astype(BF)
    ids = ids_ref[...]
    coarse = ids // 16
    pieces = (coarse, ids - 16 * coarse)
    lanes = 128
    quarters = [
        jnp.broadcast_to(piece[:, half * lanes : (half + 1) * lanes].astype(F32), (4, lanes))
        for piece in pieces
        for half in range(2)
    ]
    tile = jnp.concatenate(quarters, axis=0).astype(BF)
    for start in range(0, width, 16):
        out_ref[start : start + 16, rows:] = tile


def front_kernel(
    scale, in_ref, tab_ref, constants_hbm, parts_hbm, spectra_hbm, mixed_ref,
    constants_ref, parts_ref, spectra_ref, wide_ref, in_sems, out_sems,
):
    width, rows = mixed_ref.shape
    chans = tab_ref.shape[0] // 3
    vocab = tab_ref.shape[1]
    blocks = width // chans
    half = width // 2
    size = wide_ref.shape[2]
    constants = Constants(constants_ref, blocks, rows)
    total = constants_ref.shape[0]
    incoming = started(
        [
            pltpu.make_async_copy(constants_hbm.at[part], constants_ref.at[part], in_sems.at[place])
            for place, part in enumerate((slice(0, constants.early), slice(constants.early, total)))
        ]
    )
    query, key, value, ids = (slice(rows * part, rows * (part + 1)) for part in range(4))
    ids = slice(3 * rows, parts_ref.shape[1])
    parts_ref[:, ids] = in_ref[:, rows:]

    def body(s, carry):
        picked = mm(tab_ref[...], onehots(parts_ref.at[:, ids], s, chans, vocab)).astype(BF)
        place = pl.ds(pl.multiple_of(s * chans, chans), chans)
        parts_ref[place, query] = picked[:chans]
        parts_ref[place, key] = picked[chans : 2 * chans]
        parts_ref[place, value] = picked[2 * chans :]
        return carry

    lax.fori_loop(0, blocks, body, 0, unroll=8)
    leaving = started([pltpu.make_async_copy(parts_ref, parts_hbm, out_sems.at[0])])
    incoming[0].wait()
    spread(in_ref[:, :rows].astype(F32), wide_ref)
    fr, fi, gr, gi, cause = (slice(rows * part, rows * (part + 1)) for part in range(5))
    for group in range(2):
        place = slice(group * half, (group + 1) * half)
        spectra_ref[place, : 2 * rows] = forward(group_of(wide_ref, group), False, constants) * scale
    spread(parts_ref[:, key].astype(F32) * parts_ref[:, value].astype(F32), wide_ref)
    for group in range(2):
        place = slice(group * half, (group + 1) * half)
        spectra_ref[place, 2 * rows : 4 * rows] = forward(
            group_of(wide_ref, group), True, constants
        )
    leaving += started(
        [
            pltpu.make_async_copy(
                spectra_ref.at[:, : 4 * rows], spectra_hbm.at[:, : 4 * rows], out_sems.at[1]
            )
        ]
    )
    incoming[1].wait()
    for group in range(2):
        place = slice(group * half, (group + 1) * half)
        a, b = spectra_ref[place, fr], spectra_ref[place, fi]
        c, d = spectra_ref[place, gr], spectra_ref[place, gi]
        causal = inverse(c * a - d * b, c * b + d * a, constants)
        wide_ref[:, group] = causal.reshape(blocks, size, rows)
    causal = joined(wide_ref)
    spectra_ref[:, cause] = causal
    leaving += started(
        [
            pltpu.make_async_copy(
                spectra_ref.at[:, cause], spectra_hbm.at[:, cause], out_sems.at[2]
            )
        ]
    )
    mixed_ref[...] = (parts_ref[:, query].astype(F32) * causal).astype(BF)
    for copy in leaving:
        copy.wait()


def back_kernel(
    scale, b_ref, constants_ref, parts_ref, spectra_ref, out_ref,
    act_ref, spec_ref, acc_ref, wide_ref,
):
    width, rows = b_ref.shape
    blocks = act_ref.shape[0]
    chans = width // blocks
    vocab = acc_ref.shape[0]
    half = width // 2
    size = wide_ref.shape[2]
    shape = (blocks, chans, rows)
    constants = Constants(constants_ref, blocks, rows)
    query, key, value = (slice(rows * part, rows * (part + 1)) for part in range(3))
    ids = slice(3 * rows, parts_ref.shape[1])
    spread(b_ref[...].astype(F32) * parts_ref[:, query].astype(F32), wide_ref)
    for group in range(2):
        place = slice(group * half, (group + 1) * half)
        spec_ref[place] = forward(group_of(wide_ref, group), True, constants)

    def correlate(start):
        for group in range(2):
            place = slice(group * half, (group + 1) * half)
            cr, ci = spec_ref[place, :rows], spec_ref[place, rows:]
            xr = spectra_ref[place, start : start + rows]
            xi = spectra_ref[place, start + rows : start + 2 * rows]
            result = inverse(xr * cr + xi * ci, xr * ci - xi * cr, constants)
            wide_ref[:, group] = result.reshape(blocks, size, rows)
        return joined(wide_ref)

    out_ref[:, :rows] = (correlate(2 * rows) * scale).astype(BF)
    causal = spectra_ref[:, 4 * rows :]
    act_ref[:, :chans] = (b_ref[...].astype(F32) * causal).astype(BF).reshape(shape)
    gated_grad = correlate(0)
    act_ref[:, chans : 2 * chans] = (
        (gated_grad * parts_ref[:, value].astype(F32)).astype(BF).reshape(shape)
    )
    act_ref[:, 2 * chans :] = (
        (gated_grad * parts_ref[:, key].astype(F32)).astype(BF).reshape(shape)
    )
    acc_ref[...] = jnp.zeros_like(acc_ref)
    group = 4

    def body(step, carry):
        hot = jnp.concatenate(
            [onehots(parts_ref.at[:, ids], step * group + g, chans, vocab) for g in range(group)],
            axis=1,
        )
        act = jnp.concatenate([act_ref[step * group + g] for g in range(group)], axis=1)
        acc_ref[:, : 3 * chans] += lax.dot_general(
            hot, act, (((1,), (1,)), ((), ())), preferred_element_type=F32
        )
        return carry

    lax.fori_loop(0, blocks // group, body, 0)
    out_ref[:, rows:] = acc_ref[...].astype(BF)


def output_kernel(mixed_ref, w_hbm, out_hbm, w_ref, out_ref, in_sems, out_sems):
    chunks = w_ref.shape[0]
    lanes = w_ref.shape[2]
    incoming = started(
        [
            pltpu.make_async_copy(
                w_hbm.at[:, chunk * lanes : (chunk + 1) * lanes], w_ref.at[chunk], in_sems.at[chunk]
            )
            for chunk in range(chunks)
        ]
    )
    left = mixed_ref[...].astype(F32).T.astype(BF)
    leaving = []
    for chunk in range(chunks):
        incoming[chunk].wait()
        place = slice(chunk * lanes, (chunk + 1) * lanes)
        out_ref[:, place] = mm(left, w_ref[chunk]).astype(BF)
        leaving += started(
            [pltpu.make_async_copy(out_ref.at[:, place], out_hbm.at[:, place], out_sems.at[chunk])]
        )
    for copy in leaving:
        copy.wait()


def project_kernel(w_hbm, cot_hbm, back_ref, w_ref, cot_ref, acc_ref, w_sems, cot_sems):
    chunks = w_ref.shape[0]
    lanes = w_ref.shape[2]
    incoming = [
        (
            pltpu.make_async_copy(
                cot_hbm.at[:, chunk * lanes : (chunk + 1) * lanes],
                cot_ref.at[chunk],
                cot_sems.at[chunk],
            ),
            pltpu.make_async_copy(
                w_hbm.at[:, chunk * lanes : (chunk + 1) * lanes], w_ref.at[chunk], w_sems.at[chunk]
            ),
        )
        for chunk in range(chunks)
    ]
    for pair in incoming:
        started(pair)
    for chunk in range(chunks):
        for copy in incoming[chunk]:
            copy.wait()
        term = lax.dot_general(
            w_ref[chunk], cot_ref[chunk], (((1,), (1,)), ((), ())), preferred_element_type=F32
        )
        if chunk:
            term = acc_ref[...] + term
        if chunk < chunks - 1:
            acc_ref[...] = term
        else:
            back_ref[...] = term.astype(BF)


def finish_kernel(in_ref, grad_ref, table_ref):
    width, rows = grad_ref.shape[1], grad_ref.shape[0]
    vocab_rows = table_ref.shape[1]
    chans = vocab_rows * width // in_ref.shape[0]
    grad_ref[...] = in_ref[:, :rows].astype(F32).T
    sums = in_ref[:, rows:]
    lanes = sums.shape[1]
    column = lax.broadcasted_iota(jnp.int32, (lanes, width), 1)
    row = lax.broadcasted_iota(jnp.int32, (lanes, width), 0)
    source = lax.broadcasted_iota(jnp.int32, (width, width), 0) // vocab_rows
    mine = source == lax.broadcasted_iota(jnp.int32, (width, width), 1) // chans
    pick = lax.broadcasted_iota(jnp.int32, (vocab_rows, width), 1) % vocab_rows
    pick = pick == lax.broadcasted_iota(jnp.int32, (vocab_rows, width), 0)
    pick = pick.astype(F32).astype(BF)
    for field in range(3):
        take = (row == field * chans + column % chans).astype(F32).astype(BF)
        spreaded = jnp.where(mine, mm(sums, take), 0.0).astype(BF)
        table_ref[field] = mm(pick, spreaded)


def params(mebibytes):
    return pltpu.CompilerParams(vmem_limit_bytes=mebibytes * 1024 * 1024)


HBM = pl.BlockSpec(memory_space=pltpu.HBM)
VMEM = pl.BlockSpec(memory_space=pltpu.VMEM)
DMA = pltpu.SemaphoreType.DMA


def shards(token_ids, table, filter_raw, w_out, cotangent):
    rows = token_ids.shape[0]
    blocks = lax.axis_size("ctx")
    width, features = w_out.shape
    chans = width // blocks
    vocab = table.shape[0]
    length = rows * blocks
    position = lax.axis_index("ctx")
    scale = 1.0 / math.sqrt(length)
    constants = tables(blocks, chans // 2, rows)
    struct = jax.ShapeDtypeStruct
    field = struct((width, rows), BF)
    parts = struct((width, 3 * rows + 128), BF)
    spectra = struct((width, 5 * rows), F32)
    parcel = struct((width, rows + 128), BF)
    spread_shape = pltpu.VMEM((blocks, 2, chans // 2, rows), F32)
    chunks = 8
    lanes = features // chunks

    def exchange(values):
        return lax.all_to_all(values, "ctx", split_axis=0, concat_axis=0, tiled=True)

    sent = pl.pallas_call(
        send_kernel, out_shape=parcel, compiler_params=params(62), name="send"
    )(filter_raw, token_ids[None])
    received = exchange(sent)
    cot_full = lax.all_gather(cotangent, "tp", axis=1, tiled=True)

    local = lax.dynamic_slice(table, (0, 0, position * chans), (vocab, 3, chans))
    local = local.transpose(1, 2, 0).reshape(3 * chans, vocab)
    held, spectra_held, mixed = pl.pallas_call(
        functools.partial(front_kernel, scale),
        out_shape=(parts, spectra, field),
        in_specs=[VMEM, VMEM, HBM],
        out_specs=(HBM, HBM, VMEM),
        scratch_shapes=[
            pltpu.VMEM(constants.shape, BF),
            pltpu.VMEM(parts.shape, BF),
            pltpu.VMEM(spectra.shape, F32),
            spread_shape,
            DMA((2,)),
            DMA((3,)),
        ],
        compiler_params=params(50),
        name="front",
    )(received, local, constants)
    mixed_rows = exchange(mixed)
    partial_out = pl.pallas_call(
        output_kernel,
        out_shape=struct((rows, features), BF),
        in_specs=[VMEM, HBM],
        out_specs=HBM,
        scratch_shapes=[
            pltpu.VMEM((chunks, width, lanes), BF),
            pltpu.VMEM((rows, features), BF),
            DMA((chunks,)),
            DMA((chunks,)),
        ],
        compiler_params=params(61),
        name="project_out",
    )(mixed_rows, w_out)
    output = lax.psum_scatter(partial_out, "tp", scatter_dimension=1, tiled=True)

    back = pl.pallas_call(
        project_kernel,
        out_shape=field,
        in_specs=[HBM, HBM],
        scratch_shapes=[
            pltpu.VMEM((chunks, width, lanes), BF),
            pltpu.VMEM((chunks, rows, lanes), BF),
            pltpu.VMEM(field.shape, F32),
            DMA((chunks,)),
            DMA((chunks,)),
        ],
        compiler_params=params(54),
        name="project_back",
    )(w_out, cot_full)
    back_field = exchange(back)
    grads = pl.pallas_call(
        functools.partial(back_kernel, scale),
        out_shape=parcel,
        scratch_shapes=[
            pltpu.VMEM((blocks, 3 * chans, rows), BF),
            pltpu.VMEM((width, 2 * rows), F32),
            pltpu.VMEM((vocab, 128), F32),
            spread_shape,
        ],
        compiler_params=params(24),
        name="back",
    )(back_field, constants, held, spectra_held)
    grads = exchange(grads)
    vocab_rows = vocab // blocks
    grad_filter, grad_table = pl.pallas_call(
        finish_kernel,
        out_shape=(struct((rows, width), F32), struct((3, vocab_rows, width), F32)),
        compiler_params=params(8),
        name="finish",
    )(grads)
    return (output, grad_filter, grad_table.transpose(1, 0, 2))


def solution(mesh):
    return jax.shard_map(
        shards,
        mesh=mesh,
        in_specs=(P("ctx"), P(None, None, "tp"), P("ctx", "tp"), P("tp", None), P("ctx", "tp")),
        out_specs=(P("ctx", "tp"), P("ctx", "tp"), P("ctx", None, "tp")),
        check_vma=False,
    )
```

time: 111 us -> 109 us (0.982)
  matrix products: 8.96 us -> 0 us
  Pallas kernels: 27.1 us -> 36 us
  local copies, waits for them, and re-layouts: 1.69 us -> 0.34 us
    dot_general x2 -> x0, matrix products: 8.96 us -> none  [the longest x1 4.81 us: shards(): lax.dot_general(mixed_rows, w_out, (((0,), (0,)), ((), ())), preferred_el...]
    pallas_call x2 -> x4, Pallas kernels: 23.5 us -> 32.4 us  [the longest x1 13.4 us: shards(): pl.pallas_call(functools.partial(front_kernel, scale), out_shape=(parts,...]
  transfers between devices with their start and end apart: 3 -> 3, of which waited for: 1 -> 1; matrix products, arithmetic and copies ran while one was open for 9% -> 0% of each run, Pallas kernels for 23% -> 31%
where the time goes in v3:
time: 109 us
  blocking collectives  39.2 us (36%)
  Pallas kernels  36 us (33%)
  between operations  14.1 us (13%)
  waiting for transfers between devices  10.5 us (10%)
  starting transfers between devices  8.67 us (8%)
    all_to_all x3, blocking collectives, exchange(): lax.all_to_all(values, 'ctx', split_axis=0, concat_axis=0, tiled=True)  39.2 us
    pallas_call x1, Pallas kernels, shards(): pl.pallas_call(functools.partial(front_kernel, scale), out_shape=(parts,...  13.4 us
    all_to_all x1, waiting for transfers between devices, exchange(): lax.all_to_all(values, 'ctx', split_axis=0, concat_axis=0, tiled=True)  9.78 us
    all_to_all x1, starting transfers between devices, exchange(): lax.all_to_all(values, 'ctx', split_axis=0, concat_axis=0, tiled=True)  8.59 us
    pallas_call x1, Pallas kernels, shards(): pl.pallas_call(functools.partial(back_kernel, scale), out_shape=parcel, s...  8.56 us
    pallas_call x1, Pallas kernels, shards(): pl.pallas_call(output_kernel, out_shape=struct((rows, features), BF), in_...  5.3 us
    pallas_call x1, Pallas kernels, shards(): pl.pallas_call(project_kernel, out_shape=field, in_specs=[HBM, HBM], scra...  5.05 us
  transfers between devices with their start and end apart: 3, of which 1 were waited for; matrix products, arithmetic and copies ran while one was open for 0% of the time, Pallas kernels for 31%

profile of v3, /device:TPU:1, one launch (start us, length us, event | category | flops | bytes accessed | tf_op | source)
XLA Modules:
  0.0 108.8 jit_solution(14269500129703174465)
XLA Ops:
  7.2 0.0 copy-start
  7.2 0.0 all-gather.2.cloned.1.call-start
  7.2 0.7 all-gather.2.cloned.1.call-update
  7.9 1.9 %send.1 = bf16[512,384]{1,0:T(8,128)(2,1)} custom-call(f32[256,512]{1,0:T(8,128)} %f_ref.1, s32[1,256]{1,0:T(1,128)} %bitcast.22), custom_call_target="tpu_custom_call" | custom-call | tf_op jit(solution)/shard_map/send/pallas_call | solution.py:417
  9.8 8.6 %all-to-all-start = ((bf16[32,16,384]{2,1,0:T(8,128)(2,1)}), bf16[32,16,384]{2,1,0:T(8,128)(2,1)S(1)}, u32[]{:S(2)}, u32[]{:S(2)}) async-start(bf16[32,16,384]{2,1,0:T(8,128)(2,1)} %bitcast.19), calls=%async_computation | async-start | bytes 786432 | tf_op jit(solution)/shard_map/all_to_all | solution.py:415
  18.4 0.0 reduce-scatter.2.cloned.1.call-start
  18.5 0.0 copy-done
  18.5 0.2 dynamic-slice_bitcast_fusion
  18.7 0.1 copy.9
  18.8 9.8 %all-to-all-done = bf16[32,16,384]{2,1,0:T(8,128)(2,1)S(1)} async-done(((bf16[32,16,384]{2,1,0:T(8,128)(2,1)}), bf16[32,16,384]{2,1,0:T(8,128)(2,1)S(1)}, u32[]{:S(2)}, u32[]{:S(2)}) %all-to-all-start) | async-done | bytes 393248 | tf_op jit(solution)/shard_map/all_to_all | solution.py:415
  28.6 13.4 %front.1 = (bf16[512,896]{1,0:T(8,128)(2,1)S(1)}, f32[512,1280]{1,0:T(8,128)}, bf16[512,256]{1,0:T(8,128)(2,1)S(1)}) custom-call(bf16[512,384]{1,0:T(8,128)(2,1)S(1)} %bitcast.14, bf16[48,512]{1,0:T(8,128)(2,1)S(1)} %bitcast.18, bf16[3136,512]{1,0:T(8,128)(2,1)} %constant.14.clone.constants_hbm.constants_ref), custom_call_target="tpu_custom_call" | custom-call | tf_op jit(solution)/shard_map/front/pallas_call | solution.py:425
  42.1 12.7 %all_to_all.44 = bf16[32,16,256]{2,1,0:T(8,128)(2,1)} all-to-all(bf16[32,16,256]{2,1,0:T(8,128)(2,1)S(1)} %bitcast.17), channel_id=1, replica_groups=mesh['ctx'=32,'tp'=8] {'ctx'}, dimensions={0} | all-to-all | bytes 524288 | tf_op jit(solution)/shard_map/all_to_all | solution.py:415
  54.8 5.3 %project_out.1 = bf16[256,4096]{1,0:T(8,128)(2,1)} custom-call(bf16[512,256]{1,0:T(8,128)(2,1)} %bitcast.20, bf16[512,4096]{1,0:T(8,128)(2,1)} %w_hbm.3), custom_call_target="tpu_custom_call" | custom-call | tf_op jit(solution)/shard_map/project_out/pallas_call | solution.py:442
  60.1 0.0 reduce-scatter.2.cloned.1.call-update
  60.1 0.0 all-gather.2.cloned.1.call-done.cot_hbm
  60.1 0.0 copy-start.1
  60.1 0.0 copy-start.2
  60.1 5.0 %project_back.1 = bf16[512,256]{1,0:T(8,128)(2,1)} custom-call(bf16[512,4096]{1,0:T(8,128)(2,1)} %w_hbm.3, bf16[256,4096]{1,0:T(8,128)(2,1)} %all-gather.2.cloned.1.call-done.cot_hbm), custom_call_target="tpu_custom_call" | custom-call | tf_op jit(solution)/shard_map/project_back/pallas_call | solution.py:458
  65.2 12.8 %all_to_all.45 = bf16[32,16,256]{2,1,0:T(8,128)(2,1)S(1)} all-to-all(bf16[32,16,256]{2,1,0:T(8,128)(2,1)} %bitcast.21), channel_id=1, replica_groups=mesh['ctx'=32,'tp'=8] {'ctx'}, dimensions={0} | all-to-all | bytes 524288 | tf_op jit(solution)/shard_map/all_to_all | solution.py:415
  78.0 0.0 copy-done.1
  78.0 0.0 copy-done.2
  78.0 8.6 %back.1 = bf16[512,384]{1,0:T(8,128)(2,1)S(1)} custom-call(bf16[512,256]{1,0:T(8,128)(2,1)S(1)} %bitcast.16, bf16[3136,512]{1,0:T(8,128)(2,1)S(1)} %copy-done.1, bf16[512,896]{1,0:T(8,128)(2,1)S(1)} %get-tuple-element.9.parts_ref, f32[512,1280]{1,0:T(8,128)S(1)} %copy-done.2), custom_call_target="tpu_custom_call" | custom-call | tf_op jit(solution)/shard_map/back/pallas_call | solution.py:473
  86.6 13.7 %all_to_all.46 = bf16[32,16,384]{2,1,0:T(8,128)(2,1)S(1)} all-to-all(bf16[32,16,384]{2,1,0:T(8,128)(2,1)S(1)} %bitcast.13), channel_id=1, replica_groups=mesh['ctx'=32,'tp'=8] {'ctx'}, dimensions={0} | all-to-all | bytes 786432 | tf_op jit(solution)/shard_map/all_to_all | solution.py:415
  100.3 1.7 %finish.1 = (f32[256,512]{1,0:T(8,128)}, f32[3,16,512]{2,1,0:T(8,128)}) custom-call(bf16[512,384]{1,0:T(8,128)(2,1)S(1)} %bitcast.15), custom_call_target="tpu_custom_call" | custom-call | tf_op jit(solution)/shard_map/finish/pallas_call | solution.py:487
  (1 shorter events, 0.0 us)
Async XLA Ops:
  7.2 11.3 %copy-start = (bf16[512,3,512]{2,0,1:T(8,128)(2,1)S(1)}, bf16[512,3,512]{2,0,1:T(8,128)(2,1)}, u32[]{:S(2)}) copy-start(bf16[512,3,512]{2,0,1:T(8,128)(2,1)} %param.7) | copy-start | bytes 4718596
  7.2 52.9 %all-gather.2.cloned.1.call-start = ((), (), s32[]{:S(2)}) async-start(), calls=%async_computation.6 | async-start | bytes 2359296 | tf_op jit(solution)/shard_map/all_gather | solution.py:421
  9.8 18.8 %all-to-all-start = ((bf16[32,16,384]{2,1,0:T(8,128)(2,1)}), bf16[32,16,384]{2,1,0:T(8,128)(2,1)S(1)}, u32[]{:S(2)}, u32[]{:S(2)}) async-start(bf16[32,16,384]{2,1,0:T(8,128)(2,1)} %bitcast.19), calls=%async_computation | async-start | bytes 786432 | tf_op jit(solution)/shard_map/all_to_all | solution.py:415
  18.4 83.5 %reduce-scatter.2.cloned.1.call-start = ((), (), s32[]{:S(2)}) async-start(), calls=%async_computation.5 | async-start | bytes 2359296 | tf_op jit(solution)/shard_map/reduce_scatter | solution.py:456
  60.1 17.9 %copy-start.1 = (bf16[3136,512]{1,0:T(8,128)(2,1)S(1)}, bf16[3136,512]{1,0:T(8,128)(2,1)}, u32[]{:S(2)}) copy-start(bf16[3136,512]{1,0:T(8,128)(2,1)} %constant.14.clone.constants_hbm.constants_ref) | copy-start | bytes 9633796
  60.1 17.8 %copy-start.2 = (f32[512,1280]{1,0:T(8,128)S(1)}, f32[512,1280]{1,0:T(8,128)}, u32[]{:S(2)}) copy-start(f32[512,1280]{1,0:T(8,128)} %get-tuple-element.10.spectra_ref) | copy-start | bytes 7864324
Sparse Core Ops, SparseCore 0:
  9.8 41.5 all-gather.1
  60.2 36.6 reduce-scatter.1

commit v4 on v3

--- a/solution.py
+++ b/solution.py
@@ -201,7 +201,7 @@
     parts_ref[:, ids] = in_ref[:, rows:]
 
     def body(s, carry):
-        picked = mm(tab_ref[...], onehots(parts_ref.at[:, ids], s, chans, vocab)).astype(BF)
+        picked = mm(tab_ref[...], onehots(in_ref.at[:, rows:], s, chans, vocab)).astype(BF)
         place = pl.ds(pl.multiple_of(s * chans, chans), chans)
         parts_ref[place, query] = picked[:chans]
         parts_ref[place, key] = picked[chans : 2 * chans]
@@ -307,62 +307,6 @@
     out_ref[:, rows:] = acc_ref[...].astype(BF)
 
 
-def output_kernel(mixed_ref, w_hbm, out_hbm, w_ref, out_ref, in_sems, out_sems):
-    chunks = w_ref.shape[0]
-    lanes = w_ref.shape[2]
-    incoming = started(
-        [
-            pltpu.make_async_copy(
-                w_hbm.at[:, chunk * lanes : (chunk + 1) * lanes], w_ref.at[chunk], in_sems.at[chunk]
-            )
-            for chunk in range(chunks)
-        ]
-    )
-    left = mixed_ref[...].astype(F32).T.astype(BF)
-    leaving = []
-    for chunk in range(chunks):
-        incoming[chunk].wait()
-        place = slice(chunk * lanes, (chunk + 1) * lanes)
-        out_ref[:, place] = mm(left, w_ref[chunk]).astype(BF)
-        leaving += started(
-            [pltpu.make_async_copy(out_ref.at[:, place], out_hbm.at[:, place], out_sems.at[chunk])]
-        )
-    for copy in leaving:
-        copy.wait()
-
-
-def project_kernel(w_hbm, cot_hbm, back_ref, w_ref, cot_ref, acc_ref, w_sems, cot_sems):
-    chunks = w_ref.shape[0]
-    lanes = w_ref.shape[2]
-    incoming = [
-        (
-            pltpu.make_async_copy(
-                cot_hbm.at[:, chunk * lanes : (chunk + 1) * lanes],
-                cot_ref.at[chunk],
-                cot_sems.at[chunk],
-            ),
-            pltpu.make_async_copy(
-                w_hbm.at[:, chunk * lanes : (chunk + 1) * lanes], w_ref.at[chunk], w_sems.at[chunk]
-            ),
-        )
-        for chunk in range(chunks)
-    ]
-    for pair in incoming:
-        started(pair)
-    for chunk in range(chunks):
-        for copy in incoming[chunk]:
-            copy.wait()
-        term = lax.dot_general(
-            w_ref[chunk], cot_ref[chunk], (((1,), (1,)), ((), ())), preferred_element_type=F32
-        )
-        if chunk:
-            term = acc_ref[...] + term
-        if chunk < chunks - 1:
-            acc_ref[...] = term
-        else:
-            back_ref[...] = term.astype(BF)
-
-
 def finish_kernel(in_ref, grad_ref, table_ref):
     width, rows = grad_ref.shape[1], grad_ref.shape[0]
     vocab_rows = table_ref.shape[1]
@@ -439,36 +383,14 @@
         name="front",
     )(received, local, constants)
     mixed_rows = exchange(mixed)
-    partial_out = pl.pallas_call(
-        output_kernel,
-        out_shape=struct((rows, features), BF),
-        in_specs=[VMEM, HBM],
-        out_specs=HBM,
-        scratch_shapes=[
-            pltpu.VMEM((chunks, width, lanes), BF),
-            pltpu.VMEM((rows, features), BF),
-            DMA((chunks,)),
-            DMA((chunks,)),
-        ],
-        compiler_params=params(61),
-        name="project_out",
-    )(mixed_rows, w_out)
+    partial_out = lax.dot_general(
+        mixed_rows, w_out, (((0,), (0,)), ((), ())), preferred_element_type=F32
+    ).astype(BF)
     output = lax.psum_scatter(partial_out, "tp", scatter_dimension=1, tiled=True)
 
-    back = pl.pallas_call(
-        project_kernel,
-        out_shape=field,
-        in_specs=[HBM, HBM],
-        scratch_shapes=[
-            pltpu.VMEM((chunks, width, lanes), BF),
-            pltpu.VMEM((chunks, rows, lanes), BF),
-            pltpu.VMEM(field.shape, F32),
-            DMA((chunks,)),
-            DMA((chunks,)),
-        ],
-        compiler_params=params(54),
-        name="project_back",
-    )(w_out, cot_full)
+    back = lax.dot_general(
+        w_out, cot_full, (((1,), (1,)), ((), ())), preferred_element_type=F32
+    ).astype(BF)
     back_field = exchange(back)
     grads = pl.pallas_call(
         functools.partial(back_kernel, scale),

time: 109 us -> 107 us (0.982)
  Pallas kernels: 36 us -> 21.3 us
  matrix products: 0 us -> 9.12 us
  blocking collectives: 39.2 us -> 42.4 us
    pallas_call x2 -> x0, Pallas kernels: 10.4 us -> none  [the longest x1 5.3 us: shards(): pl.pallas_call(output_kernel, out_shape=struct((rows, features), BF), in_...]
    dot_general x0 -> x2, matrix products: none -> 9.12 us  [the longest x1 4.84 us: shards(): lax.dot_general(mixed_rows, w_out, (((0,), (0,)), ((), ())), preferred_el...]
    pallas_call x1, Pallas kernels: 13.4 us -> 9.07 us  [shards(): pl.pallas_call(functools.partial(front_kernel, scale), out_shape=(parts,...]
    all_to_all x3, blocking collectives: 39.2 us -> 42.4 us  [exchange(): lax.all_to_all(values, 'ctx', split_axis=0, concat_axis=0, tiled=True)]
  transfers between devices with their start and end apart: 3 -> 3, of which waited for: 1 -> 1; matrix products, arithmetic and copies ran while one was open for 0% -> 9% of each run, Pallas kernels for 31% -> 18%
where the time goes in v4:
time: 107 us; the launch traced here: 106 us
  blocking collectives  42.4 us (40%)
  Pallas kernels  21.3 us (20%)
  between operations  14.1 us (13%)
  waiting for transfers between devices  10.5 us (10%)
  matrix products  9.12 us (9%)
  starting transfers between devices  8.67 us (8%)
    all_to_all x3, blocking collectives, exchange(): lax.all_to_all(values, 'ctx', split_axis=0, concat_axis=0, tiled=True)  42.4 us
    all_to_all x1, waiting for transfers between devices, exchange(): lax.all_to_all(values, 'ctx', split_axis=0, concat_axis=0, tiled=True)  9.78 us
    pallas_call x1, Pallas kernels, shards(): pl.pallas_call(functools.partial(front_kernel, scale), out_shape=(parts,...  9.07 us
    all_to_all x1, starting transfers between devices, exchange(): lax.all_to_all(values, 'ctx', split_axis=0, concat_axis=0, tiled=True)  8.59 us
    pallas_call x1, Pallas kernels, shards(): pl.pallas_call(functools.partial(back_kernel, scale), out_shape=parcel, s...  8.57 us
    dot_general x1, matrix products, shards(): lax.dot_general(mixed_rows, w_out, (((0,), (0,)), ((), ())), preferred_el...  4.84 us
    dot_general x1, matrix products, shards(): lax.dot_general(w_out, cot_full, (((1,), (1,)), ((), ())), preferred_elem...  4.28 us
  transfers between devices with their start and end apart: 3, of which 1 were waited for; matrix products, arithmetic and copies ran while one was open for 9% of the time, Pallas kernels for 18%

profile of v4, /device:TPU:1, one launch (start us, length us, event | category | flops | bytes accessed | tf_op | source)
XLA Modules:
  0.0 106.5 jit_solution(11713275794460724218)
XLA Ops:
  7.2 0.0 copy-start
  7.2 0.0 all-gather.2.cloned.1.call-start
  7.2 0.7 all-gather.2.cloned.1.call-update
  7.9 1.9 %send.1 = bf16[512,384]{1,0:T(8,128)(2,1)} custom-call(f32[256,512]{1,0:T(8,128)} %f_ref.1, s32[1,256]{1,0:T(1,128)} %bitcast.26), custom_call_target="tpu_custom_call" | custom-call | tf_op jit(solution)/shard_map/send/pallas_call | solution.py:361
  9.8 8.6 %all-to-all-start = ((bf16[32,16,384]{2,1,0:T(8,128)(2,1)}), bf16[32,16,384]{2,1,0:T(8,128)(2,1)S(1)}, u32[]{:S(2)}, u32[]{:S(2)}) async-start(bf16[32,16,384]{2,1,0:T(8,128)(2,1)} %bitcast.23), calls=%async_computation | async-start | bytes 786432 | tf_op jit(solution)/shard_map/all_to_all | solution.py:359
  18.4 0.0 reduce-scatter.2.cloned.1.call-start
  18.5 0.0 copy-done
  18.5 0.2 dynamic-slice_bitcast_fusion
  18.7 0.1 copy.9
  18.8 9.8 %all-to-all-done = bf16[32,16,384]{2,1,0:T(8,128)(2,1)S(1)} async-done(((bf16[32,16,384]{2,1,0:T(8,128)(2,1)}), bf16[32,16,384]{2,1,0:T(8,128)(2,1)S(1)}, u32[]{:S(2)}, u32[]{:S(2)}) %all-to-all-start) | async-done | bytes 393248 | tf_op jit(solution)/shard_map/all_to_all | solution.py:359
  28.6 9.1 %front.1 = (bf16[512,896]{1,0:T(8,128)(2,1)S(1)}, f32[512,1280]{1,0:T(8,128)}, bf16[512,256]{1,0:T(8,128)(2,1)S(1)}) custom-call(bf16[512,384]{1,0:T(8,128)(2,1)S(1)} %bitcast.18, bf16[48,512]{1,0:T(8,128)(2,1)S(1)} %bitcast.22, bf16[3136,512]{1,0:T(8,128)(2,1)} %constant.14.clone.constants_hbm.constants_ref), custom_call_target="tpu_custom_call" | custom-call | tf_op jit(solution)/shard_map/front/pallas_call | solution.py:369
  37.7 12.5 %all_to_all.45 = bf16[32,16,256]{2,1,0:T(8,128)(2,1)S(1)} all-to-all(bf16[32,16,256]{2,1,0:T(8,128)(2,1)S(1)} %bitcast.21), channel_id=1, replica_groups=mesh['ctx'=32,'tp'=8] {'ctx'}, dimensions={0} | all-to-all | bytes 524288 | tf_op jit(solution)/shard_map/all_to_all | solution.py:359
  50.2 4.8 %convolution_convert_fusion = bf16[256,4096]{1,0:T(8,128)(2,1)} fusion(bf16[512,256]{1,0:T(8,128)(2,1)S(1)} %bitcast.24, bf16[512,4096]{1,0:T(8,128)(2,1)} %param.9), kind=kOutput, calls=%fused_computation | convolution fusion | flops 1074790400 | bytes 6553600 | tf_op jit(solution)/shard_map/dot_general | solution.py:386
  55.0 0.0 reduce-scatter.2.cloned.1.call-update
  55.0 0.0 all-gather.2.cloned.1.call-done
  55.1 0.0 copy-start.1
  55.1 0.0 copy-start.2
  55.1 4.3 %convolution_convert_fusion.1 = bf16[512,256]{1,0:T(8,128)(2,1)S(1)} fusion(bf16[512,4096]{1,0:T(8,128)(2,1)} %param.9, bf16[256,4096]{1,0:T(8,128)(2,1)} %all-gather.2.cloned.1.call-done), kind=kOutput, calls=%fused_computation.1 | convolution fusion | flops 1073872896 | bytes 6553600 | tf_op jit(solution)/shard_map/dot_general | solution.py:391
  59.4 16.2 %all_to_all.46 = bf16[32,16,256]{2,1,0:T(8,128)(2,1)S(1)} all-to-all(bf16[32,16,256]{2,1,0:T(8,128)(2,1)S(1)} %bitcast.25), channel_id=1, replica_groups=mesh['ctx'=32,'tp'=8] {'ctx'}, dimensions={0} | all-to-all | bytes 524288 | tf_op jit(solution)/shard_map/all_to_all | solution.py:359
  75.6 0.0 copy-done.1
  75.6 0.0 copy-done.2
  75.6 8.6 %back.1 = bf16[512,384]{1,0:T(8,128)(2,1)S(1)} custom-call(bf16[512,256]{1,0:T(8,128)(2,1)S(1)} %bitcast.20, bf16[3136,512]{1,0:T(8,128)(2,1)S(1)} %copy-done.1, bf16[512,896]{1,0:T(8,128)(2,1)S(1)} %get-tuple-element.9.parts_ref, f32[512,1280]{1,0:T(8,128)S(1)} %copy-done.2), custom_call_target="tpu_custom_call" | custom-call | tf_op jit(solution)/shard_map/back/pallas_call | solution.py:395
  84.2 13.7 %all_to_all.47 = bf16[32,16,384]{2,1,0:T(8,128)(2,1)S(1)} all-to-all(bf16[32,16,384]{2,1,0:T(8,128)(2,1)S(1)} %bitcast.17), channel_id=1, replica_groups=mesh['ctx'=32,'tp'=8] {'ctx'}, dimensions={0} | all-to-all | bytes 786432 | tf_op jit(solution)/shard_map/all_to_all | solution.py:359
  97.9 1.7 %finish.1 = (f32[256,512]{1,0:T(8,128)}, f32[3,16,512]{2,1,0:T(8,128)}) custom-call(bf16[512,384]{1,0:T(8,128)(2,1)S(1)} %bitcast.19), custom_call_target="tpu_custom_call" | custom-call | tf_op jit(solution)/shard_map/finish/pallas_call | solution.py:409
  (1 shorter events, 0.0 us)
Async XLA Ops:
  7.2 11.3 %copy-start = (bf16[512,3,512]{2,0,1:T(8,128)(2,1)S(1)}, bf16[512,3,512]{2,0,1:T(8,128)(2,1)}, u32[]{:S(2)}) copy-start(bf16[512,3,512]{2,0,1:T(8,128)(2,1)} %param.7) | copy-start | bytes 4718596
  7.2 47.9 %all-gather.2.cloned.1.call-start = ((), (), s32[]{:S(2)}) async-start(), calls=%async_computation.6 | async-start | bytes 2359296 | tf_op jit(solution)/shard_map/all_gather | solution.py:365
  9.8 18.8 %all-to-all-start = ((bf16[32,16,384]{2,1,0:T(8,128)(2,1)}), bf16[32,16,384]{2,1,0:T(8,128)(2,1)S(1)}, u32[]{:S(2)}, u32[]{:S(2)}) async-start(bf16[32,16,384]{2,1,0:T(8,128)(2,1)} %bitcast.23), calls=%async_computation | async-start | bytes 786432 | tf_op jit(solution)/shard_map/all_to_all | solution.py:359
  18.4 81.2 %reduce-scatter.2.cloned.1.call-start = ((), (), s32[]{:S(2)}) async-start(), calls=%async_computation.5 | async-start | bytes 2359296 | tf_op jit(solution)/shard_map/reduce_scatter | solution.py:389
  55.1 20.5 %copy-start.1 = (bf16[3136,512]{1,0:T(8,128)(2,1)S(1)}, bf16[3136,512]{1,0:T(8,128)(2,1)}, u32[]{:S(2)}) copy-start(bf16[3136,512]{1,0:T(8,128)(2,1)} %constant.14.clone.constants_hbm.constants_ref) | copy-start | bytes 9633796
  55.1 20.5 %copy-start.2 = (f32[512,1280]{1,0:T(8,128)S(1)}, f32[512,1280]{1,0:T(8,128)}, u32[]{:S(2)}) copy-start(f32[512,1280]{1,0:T(8,128)} %get-tuple-element.10.spectra_ref) | copy-start | bytes 7864324
Sparse Core Ops, SparseCore 0:
  9.8 41.2 all-gather.1
  55.2 39.1 reduce-scatter.1

commit v5 on v4

--- a/solution.py
+++ b/solution.py
@@ -303,8 +303,32 @@
         )
         return carry
 
-    lax.fori_loop(0, blocks // group, body, 0)
+    lax.fori_loop(0, blocks // group, body, 0, unroll=blocks // group)
     out_ref[:, rows:] = acc_ref[...].astype(BF)
+
+
+def output_kernel(mixed_ref, w_hbm, out_hbm, w_ref, out_ref, in_sems, out_sems):
+    chunks, _, lanes = out_ref.shape
+    pieces = in_sems.shape[0]
+    many = chunks // pieces
+    parts = [slice(part * many * lanes, (part + 1) * many * lanes) for part in range(pieces)]
+    incoming = started(
+        [
+            pltpu.make_async_copy(w_hbm.at[:, part], w_ref.at[:, part], in_sems.at[place])
+            for place, part in enumerate(parts)
+        ]
+    )
+    left = mixed_ref[...].astype(F32).T.astype(BF)
+    leaving = []
+    for chunk in range(chunks):
+        if chunk % many == 0:
+            incoming[chunk // many].wait()
+        out_ref[chunk] = mm(left, w_ref[:, chunk * lanes : (chunk + 1) * lanes]).astype(BF)
+        leaving += started(
+            [pltpu.make_async_copy(out_ref.at[chunk], out_hbm.at[chunk], out_sems.at[chunk])]
+        )
+    for copy in leaving:
+        copy.wait()
 
 
 def finish_kernel(in_ref, grad_ref, table_ref):
@@ -352,8 +376,6 @@
     spectra = struct((width, 5 * rows), F32)
     parcel = struct((width, rows + 128), BF)
     spread_shape = pltpu.VMEM((blocks, 2, chans // 2, rows), F32)
-    chunks = 8
-    lanes = features // chunks
 
     def exchange(values):
         return lax.all_to_all(values, "ctx", split_axis=0, concat_axis=0, tiled=True)
@@ -383,10 +405,24 @@
         name="front",
     )(received, local, constants)
     mixed_rows = exchange(mixed)
-    partial_out = lax.dot_general(
-        mixed_rows, w_out, (((0,), (0,)), ((), ())), preferred_element_type=F32
-    ).astype(BF)
-    output = lax.psum_scatter(partial_out, "tp", scatter_dimension=1, tiled=True)
+    blocked = struct((features // width, rows, width), BF)
+    partial_out = pl.pallas_call(
+        output_kernel,
+        out_shape=blocked,
+        in_specs=[VMEM, HBM],
+        out_specs=HBM,
+        scratch_shapes=[
+            pltpu.VMEM(w_out.shape, BF),
+            pltpu.VMEM(blocked.shape, BF),
+            DMA((4,)),
+            DMA((blocked.shape[0],)),
+        ],
+        compiler_params=params(61),
+        name="project_out",
+    )(mixed_rows, w_out)
+    output = lax.psum_scatter(
+        partial_out.reshape(-1, width), "tp", scatter_dimension=0, tiled=True
+    )
 
     back = lax.dot_general(
         w_out, cot_full, (((1,), (1,)), ((), ())), preferred_element_type=F32

time: 107 us -> 106 us (level)
  matrix products: 9.12 us -> 4.29 us
  Pallas kernels: 21.3 us -> 24.9 us
    dot_general x1 -> x0, matrix products: 4.84 us -> none  [shards(): lax.dot_general(mixed_rows, w_out, (((0,), (0,)), ((), ())), preferred_el...]
    pallas_call x0 -> x1, Pallas kernels: none -> 4.76 us  [shards(): pl.pallas_call(output_kernel, out_shape=blocked, in_specs=[VMEM, HBM], ou...]
    pallas_call x1, Pallas kernels: 8.57 us -> 7.46 us  [shards(): pl.pallas_call(functools.partial(back_kernel, scale), out_shape=parcel, s...]
  transfers between devices with their start and end apart: 3 -> 3, of which waited for: 1 -> 1; matrix products, arithmetic and copies ran while one was open for 9% -> 4% of each run, Pallas kernels for 18% -> 22%
where the time goes in v5:
time: 106 us; the launch traced here: 105 us
  blocking collectives  42.5 us (40%)
  Pallas kernels  24.9 us (23%)
  between operations  14.1 us (13%)
  waiting for transfers between devices  10.5 us (10%)
  starting transfers between devices  8.67 us (8%)
  matrix products  4.29 us (4%)
    all_to_all x3, blocking collectives, exchange(): lax.all_to_all(values, 'ctx', split_axis=0, concat_axis=0, tiled=True)  42.5 us
    all_to_all x1, waiting for transfers between devices, exchange(): lax.all_to_all(values, 'ctx', split_axis=0, concat_axis=0, tiled=True)  9.78 us
    pallas_call x1, Pallas kernels, shards(): pl.pallas_call(functools.partial(front_kernel, scale), out_shape=(parts,...  9.07 us
    all_to_all x1, starting transfers between devices, exchange(): lax.all_to_all(values, 'ctx', split_axis=0, concat_axis=0, tiled=True)  8.59 us
    pallas_call x1, Pallas kernels, shards(): pl.pallas_call(functools.partial(back_kernel, scale), out_shape=parcel, s...  7.46 us
    pallas_call x1, Pallas kernels, shards(): pl.pallas_call(output_kernel, out_shape=blocked, in_specs=[VMEM, HBM], ou...  4.76 us
    dot_general x1, matrix products, shards(): lax.dot_general(w_out, cot_full, (((1,), (1,)), ((), ())), preferred_elem...  4.29 us
  transfers between devices with their start and end apart: 3, of which 1 were waited for; matrix products, arithmetic and copies ran while one was open for 4% of the time, Pallas kernels for 22%

profile of v5, /device:TPU:1, one launch (start us, length us, event | category | flops | bytes accessed | tf_op | source)
XLA Modules:
  0.0 105.3 jit_solution(6966521656956708119)
XLA Ops:
  7.2 0.0 copy-start
  7.2 0.0 all-gather.2.cloned.1.call-start
  7.2 0.7 all-gather.2.cloned.1.call-update
  7.9 1.9 %send.1 = bf16[512,384]{1,0:T(8,128)(2,1)} custom-call(f32[256,512]{1,0:T(8,128)} %f_ref.1, s32[1,256]{1,0:T(1,128)} %bitcast.26), custom_call_target="tpu_custom_call" | custom-call | tf_op jit(solution)/shard_map/send/pallas_call | solution.py:383
  9.8 8.6 %all-to-all-start = ((bf16[32,16,384]{2,1,0:T(8,128)(2,1)}), bf16[32,16,384]{2,1,0:T(8,128)(2,1)S(1)}, u32[]{:S(2)}, u32[]{:S(2)}) async-start(bf16[32,16,384]{2,1,0:T(8,128)(2,1)} %bitcast.23), calls=%async_computation | async-start | bytes 786432 | tf_op jit(solution)/shard_map/all_to_all | solution.py:381
  18.4 0.0 reduce-scatter.2.cloned.1.call-start
  18.5 0.0 copy-done
  18.5 0.2 dynamic-slice_bitcast_fusion
  18.7 0.1 copy.9
  18.8 9.8 %all-to-all-done = bf16[32,16,384]{2,1,0:T(8,128)(2,1)S(1)} async-done(((bf16[32,16,384]{2,1,0:T(8,128)(2,1)}), bf16[32,16,384]{2,1,0:T(8,128)(2,1)S(1)}, u32[]{:S(2)}, u32[]{:S(2)}) %all-to-all-start) | async-done | bytes 393248 | tf_op jit(solution)/shard_map/all_to_all | solution.py:381
  28.6 9.1 %front.1 = (bf16[512,896]{1,0:T(8,128)(2,1)S(1)}, f32[512,1280]{1,0:T(8,128)}, bf16[512,256]{1,0:T(8,128)(2,1)S(1)}) custom-call(bf16[512,384]{1,0:T(8,128)(2,1)S(1)} %bitcast.17, bf16[48,512]{1,0:T(8,128)(2,1)S(1)} %bitcast.21, bf16[3136,512]{1,0:T(8,128)(2,1)} %constant.14.clone.constants_hbm.constants_ref), custom_call_target="tpu_custom_call" | custom-call | tf_op jit(solution)/shard_map/front/pallas_call | solution.py:391
  37.7 12.7 %all_to_all.44 = bf16[32,16,256]{2,1,0:T(8,128)(2,1)} all-to-all(bf16[32,16,256]{2,1,0:T(8,128)(2,1)S(1)} %bitcast.20), channel_id=1, replica_groups=mesh['ctx'=32,'tp'=8] {'ctx'}, dimensions={0} | all-to-all | bytes 524288 | tf_op jit(solution)/shard_map/all_to_all | solution.py:381
  50.4 4.8 %project_out.1 = bf16[8,256,512]{2,1,0:T(8,128)(2,1)} custom-call(bf16[512,256]{1,0:T(8,128)(2,1)} %bitcast.24, bf16[512,4096]{1,0:T(8,128)(2,1)} %w_hbm.1), custom_call_target="tpu_custom_call" | custom-call | tf_op jit(solution)/shard_map/project_out/pallas_call | solution.py:409
  55.1 0.0 reduce-scatter.2.cloned.1.call-update
  55.2 0.0 all-gather.2.cloned.1.call-done
  55.2 0.0 copy-start.1
  55.2 0.0 copy-start.2
  55.2 4.3 %convolution_convert_fusion = bf16[512,256]{1,0:T(8,128)(2,1)S(1)} fusion(bf16[512,4096]{1,0:T(8,128)(2,1)} %w_hbm.1, bf16[256,4096]{1,0:T(8,128)(2,1)} %all-gather.2.cloned.1.call-done), kind=kOutput, calls=%fused_computation | convolution fusion | flops 1073872896 | bytes 6553600 | tf_op jit(solution)/shard_map/dot_general | solution.py:427
  59.5 16.1 %all_to_all.45 = bf16[32,16,256]{2,1,0:T(8,128)(2,1)S(1)} all-to-all(bf16[32,16,256]{2,1,0:T(8,128)(2,1)S(1)} %bitcast.25), channel_id=1, replica_groups=mesh['ctx'=32,'tp'=8] {'ctx'}, dimensions={0} | all-to-all | bytes 524288 | tf_op jit(solution)/shard_map/all_to_all | solution.py:381
  75.6 0.0 copy-done.1
  75.6 0.0 copy-done.2
  75.6 7.5 %back.1 = bf16[512,384]{1,0:T(8,128)(2,1)S(1)} custom-call(bf16[512,256]{1,0:T(8,128)(2,1)S(1)} %bitcast.19, bf16[3136,512]{1,0:T(8,128)(2,1)S(1)} %copy-done.1, bf16[512,896]{1,0:T(8,128)(2,1)S(1)} %get-tuple-element.9.parts_ref, f32[512,1280]{1,0:T(8,128)S(1)} %copy-done.2), custom_call_target="tpu_custom_call" | custom-call | tf_op jit(solution)/shard_map/back/pallas_call | solution.py:431
  83.1 13.7 %all_to_all.46 = bf16[32,16,384]{2,1,0:T(8,128)(2,1)S(1)} all-to-all(bf16[32,16,384]{2,1,0:T(8,128)(2,1)S(1)} %bitcast.16), channel_id=1, replica_groups=mesh['ctx'=32,'tp'=8] {'ctx'}, dimensions={0} | all-to-all | bytes 786432 | tf_op jit(solution)/shard_map/all_to_all | solution.py:381
  96.8 1.7 %finish.1 = (f32[256,512]{1,0:T(8,128)}, f32[3,16,512]{2,1,0:T(8,128)}) custom-call(bf16[512,384]{1,0:T(8,128)(2,1)S(1)} %bitcast.18), custom_call_target="tpu_custom_call" | custom-call | tf_op jit(solution)/shard_map/finish/pallas_call | solution.py:445
  (1 shorter events, 0.0 us)
Async XLA Ops:
  7.2 11.3 %copy-start = (bf16[512,3,512]{2,0,1:T(8,128)(2,1)S(1)}, bf16[512,3,512]{2,0,1:T(8,128)(2,1)}, u32[]{:S(2)}) copy-start(bf16[512,3,512]{2,0,1:T(8,128)(2,1)} %param.7) | copy-start | bytes 4718596
  7.2 48.0 %all-gather.2.cloned.1.call-start = ((), (), s32[]{:S(2)}) async-start(), calls=%async_computation.6 | async-start | bytes 2359296 | tf_op jit(solution)/shard_map/all_gather | solution.py:387
  9.8 18.8 %all-to-all-start = ((bf16[32,16,384]{2,1,0:T(8,128)(2,1)}), bf16[32,16,384]{2,1,0:T(8,128)(2,1)S(1)}, u32[]{:S(2)}, u32[]{:S(2)}) async-start(bf16[32,16,384]{2,1,0:T(8,128)(2,1)} %bitcast.23), calls=%async_computation | async-start | bytes 786432 | tf_op jit(solution)/shard_map/all_to_all | solution.py:381
  18.4 80.1 %reduce-scatter.2.cloned.1.call-start = ((), (), s32[]{:S(2)}) async-start(), calls=%async_computation.5 | async-start | bytes 2359296 | tf_op jit(solution)/shard_map/reduce_scatter | solution.py:423
  55.2 20.4 %copy-start.1 = (bf16[3136,512]{1,0:T(8,128)(2,1)S(1)}, bf16[3136,512]{1,0:T(8,128)(2,1)}, u32[]{:S(2)}) copy-start(bf16[3136,512]{1,0:T(8,128)(2,1)} %constant.14.clone.constants_hbm.constants_ref) | copy-start | bytes 9633796
  55.2 20.4 %copy-start.2 = (f32[512,1280]{1,0:T(8,128)S(1)}, f32[512,1280]{1,0:T(8,128)}, u32[]{:S(2)}) copy-start(f32[512,1280]{1,0:T(8,128)} %get-tuple-element.10.spectra_ref) | copy-start | bytes 7864324
Sparse Core Ops, SparseCore 0:
  9.8 41.2 all-gather.1
  55.3 38.8 reduce-scatter.1

commit v6 on v4

--- a/solution.py
+++ b/solution.py
@@ -208,7 +208,7 @@
         parts_ref[place, value] = picked[2 * chans :]
         return carry
 
-    lax.fori_loop(0, blocks, body, 0, unroll=8)
+    lax.fori_loop(0, blocks, body, 0, unroll=blocks)
     leaving = started([pltpu.make_async_copy(parts_ref, parts_hbm, out_sems.at[0])])
     incoming[0].wait()
     spread(in_ref[:, :rows].astype(F32), wide_ref)
@@ -303,7 +303,7 @@
         )
         return carry
 
-    lax.fori_loop(0, blocks // group, body, 0)
+    lax.fori_loop(0, blocks // group, body, 0, unroll=blocks // group)
     out_ref[:, rows:] = acc_ref[...].astype(BF)
 
 
@@ -361,11 +361,12 @@
     sent = pl.pallas_call(
         send_kernel, out_shape=parcel, compiler_params=params(62), name="send"
     )(filter_raw, token_ids[None])
+    local = lax.dynamic_slice(table, (0, 0, position * chans), (vocab, 3, chans))
+    local = local.transpose(1, 2, 0).reshape(3 * chans, vocab)
+    sent, local = lax.optimization_barrier((sent, local))
     received = exchange(sent)
     cot_full = lax.all_gather(cotangent, "tp", axis=1, tiled=True)
 
-    local = lax.dynamic_slice(table, (0, 0, position * chans), (vocab, 3, chans))
-    local = local.transpose(1, 2, 0).reshape(3 * chans, vocab)
     held, spectra_held, mixed = pl.pallas_call(
         functools.partial(front_kernel, scale),
         out_shape=(parts, spectra, field),

time: 107 us -> 105 us (0.981)
  blocking collectives: 42.4 us -> 61.3 us
  waiting for transfers between devices: 10.5 us -> 0.72 us
  starting transfers between devices: 8.67 us -> 0.08 us
  matrix products: 9.12 us -> 6.94 us
    all_to_all x3 -> x4, blocking collectives: 42.4 us -> 61.3 us  [exchange(): lax.all_to_all(values, 'ctx', split_axis=0, concat_axis=0, tiled=True)]
    all_to_all x1 -> x0, waiting for transfers between devices: 9.78 us -> none  [exchange(): lax.all_to_all(values, 'ctx', split_axis=0, concat_axis=0, tiled=True)]
    all_to_all x1 -> x0, starting transfers between devices: 8.59 us -> none  [exchange(): lax.all_to_all(values, 'ctx', split_axis=0, concat_axis=0, tiled=True)]
    dot_general x1, matrix products: 4.84 us -> 2.66 us  [shards(): lax.dot_general(mixed_rows, w_out, (((0,), (0,)), ((), ())), preferred_el...]
    pallas_call x1, Pallas kernels: 8.57 us -> 7.46 us  [shards(): pl.pallas_call(functools.partial(back_kernel, scale), out_shape=parcel, s...]
  transfers between devices with their start and end apart: 3 -> 2, of which waited for: 1 -> 0; matrix products, arithmetic and copies ran while one was open for 9% -> 7% of each run, Pallas kernels for 18% -> 18%
where the time goes in v6:
time: 105 us
  blocking collectives  61.3 us (58%)
  Pallas kernels  20.9 us (20%)
  between operations  14.1 us (13%)
  matrix products  6.94 us (7%)
    all_to_all x4, blocking collectives, exchange(): lax.all_to_all(values, 'ctx', split_axis=0, concat_axis=0, tiled=True)  61.3 us
    pallas_call x1, Pallas kernels, shards(): pl.pallas_call(functools.partial(front_kernel, scale), out_shape=(parts,...  9.77 us
    pallas_call x1, Pallas kernels, shards(): pl.pallas_call(functools.partial(back_kernel, scale), out_shape=parcel, s...  7.46 us
    dot_general x1, matrix products, shards(): lax.dot_general(w_out, cot_full, (((1,), (1,)), ((), ())), preferred_elem...  4.28 us
    dot_general x1, matrix products, shards(): lax.dot_general(mixed_rows, w_out, (((0,), (0,)), ((), ())), preferred_el...  2.66 us
  transfers between devices with their start and end apart: 2, of which 0 were waited for; matrix products, arithmetic and copies ran while one was open for 7% of the time, Pallas kernels for 18%

profile of v6, /device:TPU:1, one launch (start us, length us, event | category | flops | bytes accessed | tf_op | source)
XLA Modules:
  0.0 105.0 jit_solution(9410795006390183891)
XLA Ops:
  7.2 0.0 copy-start
  7.2 0.0 all-gather.2.cloned.1.call-start
  7.2 0.7 all-gather.2.cloned.1.call-update
  7.9 0.0 reduce-scatter.2.cloned.1.call-start
  8.0 0.6 copy-done
  8.6 0.2 dynamic-slice_bitcast_fusion
  8.8 0.1 copy.9
  8.9 1.9 %send.1 = bf16[512,384]{1,0:T(8,128)(2,1)} custom-call(f32[256,512]{1,0:T(8,128)} %f_ref.1, s32[1,256]{1,0:T(1,128)} %bitcast.26), custom_call_target="tpu_custom_call" | custom-call | tf_op jit(solution)/shard_map/send/pallas_call | solution.py:361
  10.8 19.0 %all_to_all.45 = bf16[32,16,384]{2,1,0:T(8,128)(2,1)S(1)} all-to-all(bf16[32,16,384]{2,1,0:T(8,128)(2,1)} %bitcast.23), channel_id=1, replica_groups=mesh['ctx'=32,'tp'=8] {'ctx'}, dimensions={0} | all-to-all | bytes 786432 | tf_op jit(solution)/shard_map/all_to_all | solution.py:359
  29.9 9.8 %front.1 = (bf16[512,896]{1,0:T(8,128)(2,1)S(1)}, f32[512,1280]{1,0:T(8,128)}, bf16[512,256]{1,0:T(8,128)(2,1)S(1)}) custom-call(bf16[512,384]{1,0:T(8,128)(2,1)S(1)} %bitcast.18, bf16[48,512]{1,0:T(8,128)(2,1)S(1)} %bitcast.22, bf16[3136,512]{1,0:T(8,128)(2,1)} %constant.14.clone.constants_hbm.constants_ref), custom_call_target="tpu_custom_call" | custom-call | tf_op jit(solution)/shard_map/front/pallas_call | solution.py:370
  39.6 12.5 %all_to_all.46 = bf16[32,16,256]{2,1,0:T(8,128)(2,1)S(1)} all-to-all(bf16[32,16,256]{2,1,0:T(8,128)(2,1)S(1)} %bitcast.21), channel_id=1, replica_groups=mesh['ctx'=32,'tp'=8] {'ctx'}, dimensions={0} | all-to-all | bytes 524288 | tf_op jit(solution)/shard_map/all_to_all | solution.py:359
  52.1 0.0 copy-done.3
  52.1 2.7 %convolution_convert_fusion = bf16[256,4096]{1,0:T(8,128)(2,1)} fusion(bf16[512,256]{1,0:T(8,128)(2,1)S(1)} %bitcast.24, bf16[512,4096]{1,0:T(8,128)(2,1)S(1)} %copy-done.3), kind=kOutput, calls=%fused_computation | convolution fusion | flops 1074790400 | bytes 6553600 | tf_op jit(solution)/shard_map/dot_general | solution.py:387
  54.8 0.0 reduce-scatter.2.cloned.1.call-update
  54.8 0.0 all-gather.2.cloned.1.call-done
  54.8 0.0 copy-start.1
  54.8 0.0 copy-start.2
  54.8 4.3 %convolution_convert_fusion.1 = bf16[512,256]{1,0:T(8,128)(2,1)S(1)} fusion(bf16[512,4096]{1,0:T(8,128)(2,1)} %param.9, bf16[256,4096]{1,0:T(8,128)(2,1)} %all-gather.2.cloned.1.call-done), kind=kOutput, calls=%fused_computation.1 | convolution fusion | flops 1073872896 | bytes 6553600 | tf_op jit(solution)/shard_map/dot_general | solution.py:392
  59.1 16.1 %all_to_all.47 = bf16[32,16,256]{2,1,0:T(8,128)(2,1)S(1)} all-to-all(bf16[32,16,256]{2,1,0:T(8,128)(2,1)S(1)} %bitcast.25), channel_id=1, replica_groups=mesh['ctx'=32,'tp'=8] {'ctx'}, dimensions={0} | all-to-all | bytes 524288 | tf_op jit(solution)/shard_map/all_to_all | solution.py:359
  75.3 0.0 copy-done.1
  75.3 0.0 copy-done.2
  75.3 7.5 %back.1 = bf16[512,384]{1,0:T(8,128)(2,1)S(1)} custom-call(bf16[512,256]{1,0:T(8,128)(2,1)S(1)} %bitcast.20, bf16[3136,512]{1,0:T(8,128)(2,1)S(1)} %copy-done.1, bf16[512,896]{1,0:T(8,128)(2,1)S(1)} %get-tuple-element.13.parts_ref, f32[512,1280]{1,0:T(8,128)S(1)} %copy-done.2), custom_call_target="tpu_custom_call" | custom-call | tf_op jit(solution)/shard_map/back/pallas_call | solution.py:396
  82.7 13.7 %all_to_all.48 = bf16[32,16,384]{2,1,0:T(8,128)(2,1)S(1)} all-to-all(bf16[32,16,384]{2,1,0:T(8,128)(2,1)S(1)} %bitcast.17), channel_id=1, replica_groups=mesh['ctx'=32,'tp'=8] {'ctx'}, dimensions={0} | all-to-all | bytes 786432 | tf_op jit(solution)/shard_map/all_to_all | solution.py:359
  96.5 1.7 %finish.1 = (f32[256,512]{1,0:T(8,128)}, f32[3,16,512]{2,1,0:T(8,128)}) custom-call(bf16[512,384]{1,0:T(8,128)(2,1)S(1)} %bitcast.19), custom_call_target="tpu_custom_call" | custom-call | tf_op jit(solution)/shard_map/finish/pallas_call | solution.py:410
  (2 shorter events, 0.0 us)
Async XLA Ops:
  7.2 1.4 %copy-start = (bf16[512,3,512]{2,0,1:T(8,128)(2,1)S(1)}, bf16[512,3,512]{2,0,1:T(8,128)(2,1)}, u32[]{:S(2)}) copy-start(bf16[512,3,512]{2,0,1:T(8,128)(2,1)} %param.7) | copy-start | bytes 4718596
  7.2 47.6 %all-gather.2.cloned.1.call-start = ((), (), s32[]{:S(2)}) async-start(), calls=%async_computation.6 | async-start | bytes 2359296 | tf_op jit(solution)/shard_map/all_gather | solution.py:368
  7.9 90.2 %reduce-scatter.2.cloned.1.call-start = ((), (), s32[]{:S(2)}) async-start(), calls=%async_computation.5 | async-start | bytes 2359296 | tf_op jit(solution)/shard_map/reduce_scatter | solution.py:390
  10.8 41.3 %copy-start.3 = (bf16[512,4096]{1,0:T(8,128)(2,1)S(1)}, bf16[512,4096]{1,0:T(8,128)(2,1)}, u32[]{:S(2)}) copy-start(bf16[512,4096]{1,0:T(8,128)(2,1)} %param.9) | copy-start | bytes 12582916
  54.8 20.4 %copy-start.1 = (bf16[3136,512]{1,0:T(8,128)(2,1)S(1)}, bf16[3136,512]{1,0:T(8,128)(2,1)}, u32[]{:S(2)}) copy-start(bf16[3136,512]{1,0:T(8,128)(2,1)} %constant.14.clone.constants_hbm.constants_ref) | copy-start | bytes 9633796
  54.8 20.4 %copy-start.2 = (f32[512,1280]{1,0:T(8,128)S(1)}, f32[512,1280]{1,0:T(8,128)}, u32[]{:S(2)}) copy-start(f32[512,1280]{1,0:T(8,128)} %get-tuple-element.14.spectra_ref) | copy-start | bytes 7864324
Sparse Core Ops, SparseCore 0:
  9.8 41.2 all-gather.1
  54.9 39.2 reduce-scatter.1

commit v7 on v6

--- a/solution.py
+++ b/solution.py
@@ -208,7 +208,7 @@
         parts_ref[place, value] = picked[2 * chans :]
         return carry
 
-    lax.fori_loop(0, blocks, body, 0, unroll=blocks)
+    lax.fori_loop(0, blocks, body, 0, unroll=8)
     leaving = started([pltpu.make_async_copy(parts_ref, parts_hbm, out_sems.at[0])])
     incoming[0].wait()
     spread(in_ref[:, :rows].astype(F32), wide_ref)
@@ -361,6 +361,7 @@
     sent = pl.pallas_call(
         send_kernel, out_shape=parcel, compiler_params=params(62), name="send"
     )(filter_raw, token_ids[None])
+    sent, table = lax.optimization_barrier((sent, table))
     local = lax.dynamic_slice(table, (0, 0, position * chans), (vocab, 3, chans))
     local = local.transpose(1, 2, 0).reshape(3 * chans, vocab)
     sent, local = lax.optimization_barrier((sent, local))

time: 105 us -> 105 us (level)
  blocking collectives: 61.3 us -> 62.8 us
    all_to_all x4, blocking collectives: 61.3 us -> 62.8 us  [exchange(): lax.all_to_all(values, 'ctx', split_axis=0, concat_axis=0, tiled=True)]
  transfers between devices with their start and end apart: 2 -> 2, of which waited for: 0 -> 0; matrix products, arithmetic and copies ran while one was open for 7% -> 7% of each run, Pallas kernels for 18% -> 17%
where the time goes in v7:
time: 105 us
  blocking collectives  62.8 us (60%)
  Pallas kernels  20.2 us (19%)
  between operations  14.1 us (13%)
  matrix products  6.94 us (7%)
    all_to_all x4, blocking collectives, exchange(): lax.all_to_all(values, 'ctx', split_axis=0, concat_axis=0, tiled=True)  62.8 us
    pallas_call x1, Pallas kernels, shards(): pl.pallas_call(functools.partial(front_kernel, scale), out_shape=(parts,...  9.08 us
    pallas_call x1, Pallas kernels, shards(): pl.pallas_call(functools.partial(back_kernel, scale), out_shape=parcel, s...  7.46 us
    dot_general x1, matrix products, shards(): lax.dot_general(w_out, cot_full, (((1,), (1,)), ((), ())), preferred_elem...  4.28 us
    dot_general x1, matrix products, shards(): lax.dot_general(mixed_rows, w_out, (((0,), (0,)), ((), ())), preferred_el...  2.66 us
  transfers between devices with their start and end apart: 2, of which 0 were waited for; matrix products, arithmetic and copies ran while one was open for 7% of the time, Pallas kernels for 17%

profile of v7, /device:TPU:1, one launch (start us, length us, event | category | flops | bytes accessed | tf_op | source)
XLA Modules:
  0.0 105.2 jit_solution(5341098578716862392)
XLA Ops:
  7.2 0.0 copy-start
  7.2 0.0 all-gather.2.cloned.1.call-start
  7.2 0.7 all-gather.2.cloned.1.call-update
  7.9 0.0 reduce-scatter.2.cloned.1.call-start
  8.0 1.9 %send.1 = bf16[512,384]{1,0:T(8,128)(2,1)} custom-call(f32[256,512]{1,0:T(8,128)} %f_ref.1, s32[1,256]{1,0:T(1,128)} %bitcast.26), custom_call_target="tpu_custom_call" | custom-call | tf_op jit(solution)/shard_map/send/pallas_call | solution.py:361
  9.9 0.0 copy-done
  9.9 0.2 dynamic-slice_bitcast_fusion
  10.1 0.1 copy.9
  10.2 19.0 %all_to_all.45 = bf16[32,16,384]{2,1,0:T(8,128)(2,1)S(1)} all-to-all(bf16[32,16,384]{2,1,0:T(8,128)(2,1)} %bitcast.23), channel_id=1, replica_groups=mesh['ctx'=32,'tp'=8] {'ctx'}, dimensions={0} | all-to-all | bytes 786432 | tf_op jit(solution)/shard_map/all_to_all | solution.py:359
  29.3 9.1 %front.1 = (bf16[512,896]{1,0:T(8,128)(2,1)S(1)}, f32[512,1280]{1,0:T(8,128)}, bf16[512,256]{1,0:T(8,128)(2,1)S(1)}) custom-call(bf16[512,384]{1,0:T(8,128)(2,1)S(1)} %bitcast.18, bf16[48,512]{1,0:T(8,128)(2,1)S(1)} %bitcast.22, bf16[3136,512]{1,0:T(8,128)(2,1)} %constant.14.clone.constants_hbm.constants_ref), custom_call_target="tpu_custom_call" | custom-call | tf_op jit(solution)/shard_map/front/pallas_call | solution.py:371
  38.3 12.5 %all_to_all.46 = bf16[32,16,256]{2,1,0:T(8,128)(2,1)S(1)} all-to-all(bf16[32,16,256]{2,1,0:T(8,128)(2,1)S(1)} %bitcast.21), channel_id=1, replica_groups=mesh['ctx'=32,'tp'=8] {'ctx'}, dimensions={0} | all-to-all | bytes 524288 | tf_op jit(solution)/shard_map/all_to_all | solution.py:359
  50.8 0.0 copy-done.3
  50.8 2.7 %convolution_convert_fusion = bf16[256,4096]{1,0:T(8,128)(2,1)} fusion(bf16[512,256]{1,0:T(8,128)(2,1)S(1)} %bitcast.24, bf16[512,4096]{1,0:T(8,128)(2,1)S(1)} %copy-done.3), kind=kOutput, calls=%fused_computation | convolution fusion | flops 1074790400 | bytes 6553600 | tf_op jit(solution)/shard_map/dot_general | solution.py:388
  53.5 0.0 reduce-scatter.2.cloned.1.call-update
  53.5 0.0 all-gather.2.cloned.1.call-done
  53.5 0.0 copy-start.1
  53.5 0.0 copy-start.2
  53.6 4.3 %convolution_convert_fusion.1 = bf16[512,256]{1,0:T(8,128)(2,1)S(1)} fusion(bf16[512,4096]{1,0:T(8,128)(2,1)} %param.9, bf16[256,4096]{1,0:T(8,128)(2,1)} %all-gather.2.cloned.1.call-done), kind=kOutput, calls=%fused_computation.1 | convolution fusion | flops 1073872896 | bytes 6553600 | tf_op jit(solution)/shard_map/dot_general | solution.py:393
  57.8 17.6 %all_to_all.47 = bf16[32,16,256]{2,1,0:T(8,128)(2,1)S(1)} all-to-all(bf16[32,16,256]{2,1,0:T(8,128)(2,1)S(1)} %bitcast.25), channel_id=1, replica_groups=mesh['ctx'=32,'tp'=8] {'ctx'}, dimensions={0} | all-to-all | bytes 524288 | tf_op jit(solution)/shard_map/all_to_all | solution.py:359
  75.4 0.0 copy-done.1
  75.4 0.0 copy-done.2
  75.4 7.5 %back.1 = bf16[512,384]{1,0:T(8,128)(2,1)S(1)} custom-call(bf16[512,256]{1,0:T(8,128)(2,1)S(1)} %bitcast.20, bf16[3136,512]{1,0:T(8,128)(2,1)S(1)} %copy-done.1, bf16[512,896]{1,0:T(8,128)(2,1)S(1)} %get-tuple-element.17.parts_ref, f32[512,1280]{1,0:T(8,128)S(1)} %copy-done.2), custom_call_target="tpu_custom_call" | custom-call | tf_op jit(solution)/shard_map/back/pallas_call | solution.py:397
  82.9 13.7 %all_to_all.48 = bf16[32,16,384]{2,1,0:T(8,128)(2,1)S(1)} all-to-all(bf16[32,16,384]{2,1,0:T(8,128)(2,1)S(1)} %bitcast.17), channel_id=1, replica_groups=mesh['ctx'=32,'tp'=8] {'ctx'}, dimensions={0} | all-to-all | bytes 786432 | tf_op jit(solution)/shard_map/all_to_all | solution.py:359
  96.6 1.7 %finish.1 = (f32[256,512]{1,0:T(8,128)}, f32[3,16,512]{2,1,0:T(8,128)}) custom-call(bf16[512,384]{1,0:T(8,128)(2,1)S(1)} %bitcast.19), custom_call_target="tpu_custom_call" | custom-call | tf_op jit(solution)/shard_map/finish/pallas_call | solution.py:411
  (2 shorter events, 0.0 us)
Async XLA Ops:
  7.2 2.7 %copy-start = (bf16[512,3,512]{2,0,1:T(8,128)(2,1)S(1)}, bf16[512,3,512]{2,0,1:T(8,128)(2,1)}, u32[]{:S(2)}) copy-start(bf16[512,3,512]{2,0,1:T(8,128)(2,1)} %param.7) | copy-start | bytes 4718596
  7.2 46.3 %all-gather.2.cloned.1.call-start = ((), (), s32[]{:S(2)}) async-start(), calls=%async_computation.6 | async-start | bytes 2359296 | tf_op jit(solution)/shard_map/all_gather | solution.py:369
  7.9 90.4 %reduce-scatter.2.cloned.1.call-start = ((), (), s32[]{:S(2)}) async-start(), calls=%async_computation.5 | async-start | bytes 2359296 | tf_op jit(solution)/shard_map/reduce_scatter | solution.py:391
  10.2 40.6 %copy-start.3 = (bf16[512,4096]{1,0:T(8,128)(2,1)S(1)}, bf16[512,4096]{1,0:T(8,128)(2,1)}, u32[]{:S(2)}) copy-start(bf16[512,4096]{1,0:T(8,128)(2,1)} %param.9) | copy-start | bytes 12582916
  53.5 21.9 %copy-start.1 = (bf16[3136,512]{1,0:T(8,128)(2,1)S(1)}, bf16[3136,512]{1,0:T(8,128)(2,1)}, u32[]{:S(2)}) copy-start(bf16[3136,512]{1,0:T(8,128)(2,1)} %constant.14.clone.constants_hbm.constants_ref) | copy-start | bytes 9633796
  53.5 21.9 %copy-start.2 = (f32[512,1280]{1,0:T(8,128)S(1)}, f32[512,1280]{1,0:T(8,128)}, u32[]{:S(2)}) copy-start(f32[512,1280]{1,0:T(8,128)} %get-tuple-element.18.spectra_ref) | copy-start | bytes 7864324
Sparse Core Ops, SparseCore 0:
  9.8 41.2 all-gather.1
  54.2 40.2 reduce-scatter.1

commit v8 on v7

--- a/solution.py
+++ b/solution.py
@@ -290,7 +290,7 @@
         (gated_grad * parts_ref[:, key].astype(F32)).astype(BF).reshape(shape)
     )
     acc_ref[...] = jnp.zeros_like(acc_ref)
-    group = 4
+    group = 8
 
     def body(step, carry):
         hot = jnp.concatenate(

time: 105 us -> 105 us (level)
  no operation moved by 1% of the time
where the time goes in v8:
time: 105 us
  blocking collectives  62.8 us (60%)
  Pallas kernels  20.2 us (19%)
  between operations  14.1 us (13%)
  matrix products  6.94 us (7%)
    all_to_all x4, blocking collectives, exchange(): lax.all_to_all(values, 'ctx', split_axis=0, concat_axis=0, tiled=True)  62.8 us
    pallas_call x1, Pallas kernels, shards(): pl.pallas_call(functools.partial(front_kernel, scale), out_shape=(parts,...  9.08 us
    pallas_call x1, Pallas kernels, shards(): pl.pallas_call(functools.partial(back_kernel, scale), out_shape=parcel, s...  7.46 us
    dot_general x1, matrix products, shards(): lax.dot_general(w_out, cot_full, (((1,), (1,)), ((), ())), preferred_elem...  4.28 us
    dot_general x1, matrix products, shards(): lax.dot_general(mixed_rows, w_out, (((0,), (0,)), ((), ())), preferred_el...  2.66 us
  transfers between devices with their start and end apart: 2, of which 0 were waited for; matrix products, arithmetic and copies ran while one was open for 7% of the time, Pallas kernels for 17%

profile of v8, /device:TPU:1, one launch (start us, length us, event | category | flops | bytes accessed | tf_op | source)
XLA Modules:
  0.0 105.2 jit_solution(14295547722002061964)
XLA Ops:
  7.2 0.0 copy-start
  7.2 0.0 all-gather.2.cloned.1.call-start
  7.2 0.7 all-gather.2.cloned.1.call-update
  7.9 0.0 reduce-scatter.2.cloned.1.call-start
  8.0 1.9 %send.1 = bf16[512,384]{1,0:T(8,128)(2,1)} custom-call(f32[256,512]{1,0:T(8,128)} %f_ref.1, s32[1,256]{1,0:T(1,128)} %bitcast.26), custom_call_target="tpu_custom_call" | custom-call | tf_op jit(solution)/shard_map/send/pallas_call | solution.py:361
  9.9 0.0 copy-done
  9.9 0.2 dynamic-slice_bitcast_fusion
  10.1 0.1 copy.9
  10.2 19.0 %all_to_all.45 = bf16[32,16,384]{2,1,0:T(8,128)(2,1)S(1)} all-to-all(bf16[32,16,384]{2,1,0:T(8,128)(2,1)} %bitcast.23), channel_id=1, replica_groups=mesh['ctx'=32,'tp'=8] {'ctx'}, dimensions={0} | all-to-all | bytes 786432 | tf_op jit(solution)/shard_map/all_to_all | solution.py:359
  29.3 9.1 %front.1 = (bf16[512,896]{1,0:T(8,128)(2,1)S(1)}, f32[512,1280]{1,0:T(8,128)}, bf16[512,256]{1,0:T(8,128)(2,1)S(1)}) custom-call(bf16[512,384]{1,0:T(8,128)(2,1)S(1)} %bitcast.18, bf16[48,512]{1,0:T(8,128)(2,1)S(1)} %bitcast.22, bf16[3136,512]{1,0:T(8,128)(2,1)} %constant.14.clone.constants_hbm.constants_ref), custom_call_target="tpu_custom_call" | custom-call | tf_op jit(solution)/shard_map/front/pallas_call | solution.py:371
  38.3 12.5 %all_to_all.46 = bf16[32,16,256]{2,1,0:T(8,128)(2,1)S(1)} all-to-all(bf16[32,16,256]{2,1,0:T(8,128)(2,1)S(1)} %bitcast.21), channel_id=1, replica_groups=mesh['ctx'=32,'tp'=8] {'ctx'}, dimensions={0} | all-to-all | bytes 524288 | tf_op jit(solution)/shard_map/all_to_all | solution.py:359
  50.8 0.0 copy-done.3
  50.8 2.7 %convolution_convert_fusion = bf16[256,4096]{1,0:T(8,128)(2,1)} fusion(bf16[512,256]{1,0:T(8,128)(2,1)S(1)} %bitcast.24, bf16[512,4096]{1,0:T(8,128)(2,1)S(1)} %copy-done.3), kind=kOutput, calls=%fused_computation | convolution fusion | flops 1074790400 | bytes 6553600 | tf_op jit(solution)/shard_map/dot_general | solution.py:388
  53.5 0.0 reduce-scatter.2.cloned.1.call-update
  53.5 0.0 all-gather.2.cloned.1.call-done
  53.5 0.0 copy-start.1
  53.5 0.0 copy-start.2
  53.6 4.3 %convolution_convert_fusion.1 = bf16[512,256]{1,0:T(8,128)(2,1)S(1)} fusion(bf16[512,4096]{1,0:T(8,128)(2,1)} %param.9, bf16[256,4096]{1,0:T(8,128)(2,1)} %all-gather.2.cloned.1.call-done), kind=kOutput, calls=%fused_computation.1 | convolution fusion | flops 1073872896 | bytes 6553600 | tf_op jit(solution)/shard_map/dot_general | solution.py:393
  57.8 17.6 %all_to_all.47 = bf16[32,16,256]{2,1,0:T(8,128)(2,1)S(1)} all-to-all(bf16[32,16,256]{2,1,0:T(8,128)(2,1)S(1)} %bitcast.25), channel_id=1, replica_groups=mesh['ctx'=32,'tp'=8] {'ctx'}, dimensions={0} | all-to-all | bytes 524288 | tf_op jit(solution)/shard_map/all_to_all | solution.py:359
  75.4 0.0 copy-done.1
  75.4 0.0 copy-done.2
  75.4 7.5 %back.1 = bf16[512,384]{1,0:T(8,128)(2,1)S(1)} custom-call(bf16[512,256]{1,0:T(8,128)(2,1)S(1)} %bitcast.20, bf16[3136,512]{1,0:T(8,128)(2,1)S(1)} %copy-done.1, bf16[512,896]{1,0:T(8,128)(2,1)S(1)} %get-tuple-element.17.parts_ref, f32[512,1280]{1,0:T(8,128)S(1)} %copy-done.2), custom_call_target="tpu_custom_call" | custom-call | tf_op jit(solution)/shard_map/back/pallas_call | solution.py:397
  82.9 13.7 %all_to_all.48 = bf16[32,16,384]{2,1,0:T(8,128)(2,1)S(1)} all-to-all(bf16[32,16,384]{2,1,0:T(8,128)(2,1)S(1)} %bitcast.17), channel_id=1, replica_groups=mesh['ctx'=32,'tp'=8] {'ctx'}, dimensions={0} | all-to-all | bytes 786432 | tf_op jit(solution)/shard_map/all_to_all | solution.py:359
  96.6 1.7 %finish.1 = (f32[256,512]{1,0:T(8,128)}, f32[3,16,512]{2,1,0:T(8,128)}) custom-call(bf16[512,384]{1,0:T(8,128)(2,1)S(1)} %bitcast.19), custom_call_target="tpu_custom_call" | custom-call | tf_op jit(solution)/shard_map/finish/pallas_call | solution.py:411
  (2 shorter events, 0.0 us)
Async XLA Ops:
  7.2 2.7 %copy-start = (bf16[512,3,512]{2,0,1:T(8,128)(2,1)S(1)}, bf16[512,3,512]{2,0,1:T(8,128)(2,1)}, u32[]{:S(2)}) copy-start(bf16[512,3,512]{2,0,1:T(8,128)(2,1)} %param.7) | copy-start | bytes 4718596
  7.2 46.3 %all-gather.2.cloned.1.call-start = ((), (), s32[]{:S(2)}) async-start(), calls=%async_computation.6 | async-start | bytes 2359296 | tf_op jit(solution)/shard_map/all_gather | solution.py:369
  7.9 90.4 %reduce-scatter.2.cloned.1.call-start = ((), (), s32[]{:S(2)}) async-start(), calls=%async_computation.5 | async-start | bytes 2359296 | tf_op jit(solution)/shard_map/reduce_scatter | solution.py:391
  10.2 40.6 %copy-start.3 = (bf16[512,4096]{1,0:T(8,128)(2,1)S(1)}, bf16[512,4096]{1,0:T(8,128)(2,1)}, u32[]{:S(2)}) copy-start(bf16[512,4096]{1,0:T(8,128)(2,1)} %param.9) | copy-start | bytes 12582916
  53.5 21.9 %copy-start.1 = (bf16[3136,512]{1,0:T(8,128)(2,1)S(1)}, bf16[3136,512]{1,0:T(8,128)(2,1)}, u32[]{:S(2)}) copy-start(bf16[3136,512]{1,0:T(8,128)(2,1)} %constant.14.clone.constants_hbm.constants_ref) | copy-start | bytes 9633796
  53.5 21.9 %copy-start.2 = (f32[512,1280]{1,0:T(8,128)S(1)}, f32[512,1280]{1,0:T(8,128)}, u32[]{:S(2)}) copy-start(f32[512,1280]{1,0:T(8,128)} %get-tuple-element.18.spectra_ref) | copy-start | bytes 7864324
Sparse Core Ops, SparseCore 0:
  9.8 41.2 all-gather.1
  54.2 40.2 reduce-scatter.1

commit v9 on v8

--- a/solution.py
+++ b/solution.py
@@ -290,7 +290,7 @@
         (gated_grad * parts_ref[:, key].astype(F32)).astype(BF).reshape(shape)
     )
     acc_ref[...] = jnp.zeros_like(acc_ref)
-    group = 8
+    group = 16
 
     def body(step, carry):
         hot = jnp.concatenate(

time: 105 us -> 105 us (level)
  no operation moved by 1% of the time
where the time goes in v9:
time: 105 us
  blocking collectives  62.8 us (60%)
  Pallas kernels  20.2 us (19%)
  between operations  14.1 us (13%)
  matrix products  6.94 us (7%)
    all_to_all x4, blocking collectives, exchange(): lax.all_to_all(values, 'ctx', split_axis=0, concat_axis=0, tiled=True)  62.8 us
    pallas_call x1, Pallas kernels, shards(): pl.pallas_call(functools.partial(front_kernel, scale), out_shape=(parts,...  9.08 us
    pallas_call x1, Pallas kernels, shards(): pl.pallas_call(functools.partial(back_kernel, scale), out_shape=parcel, s...  7.46 us
    dot_general x1, matrix products, shards(): lax.dot_general(w_out, cot_full, (((1,), (1,)), ((), ())), preferred_elem...  4.28 us
    dot_general x1, matrix products, shards(): lax.dot_general(mixed_rows, w_out, (((0,), (0,)), ((), ())), preferred_el...  2.66 us
  transfers between devices with their start and end apart: 2, of which 0 were waited for; matrix products, arithmetic and copies ran while one was open for 7% of the time, Pallas kernels for 17%

profile of v9, /device:TPU:1, one launch (start us, length us, event | category | flops | bytes accessed | tf_op | source)
XLA Modules:
  0.0 105.2 jit_solution(1137076040076103984)
XLA Ops:
  7.2 0.0 copy-start
  7.2 0.0 all-gather.2.cloned.1.call-start
  7.2 0.7 all-gather.2.cloned.1.call-update
  7.9 0.0 reduce-scatter.2.cloned.1.call-start
  8.0 1.9 %send.1 = bf16[512,384]{1,0:T(8,128)(2,1)} custom-call(f32[256,512]{1,0:T(8,128)} %f_ref.1, s32[1,256]{1,0:T(1,128)} %bitcast.26), custom_call_target="tpu_custom_call" | custom-call | tf_op jit(solution)/shard_map/send/pallas_call | solution.py:361
  9.9 0.0 copy-done
  9.9 0.2 dynamic-slice_bitcast_fusion
  10.1 0.1 copy.9
  10.2 19.0 %all_to_all.45 = bf16[32,16,384]{2,1,0:T(8,128)(2,1)S(1)} all-to-all(bf16[32,16,384]{2,1,0:T(8,128)(2,1)} %bitcast.23), channel_id=1, replica_groups=mesh['ctx'=32,'tp'=8] {'ctx'}, dimensions={0} | all-to-all | bytes 786432 | tf_op jit(solution)/shard_map/all_to_all | solution.py:359
  29.3 9.1 %front.1 = (bf16[512,896]{1,0:T(8,128)(2,1)S(1)}, f32[512,1280]{1,0:T(8,128)}, bf16[512,256]{1,0:T(8,128)(2,1)S(1)}) custom-call(bf16[512,384]{1,0:T(8,128)(2,1)S(1)} %bitcast.18, bf16[48,512]{1,0:T(8,128)(2,1)S(1)} %bitcast.22, bf16[3136,512]{1,0:T(8,128)(2,1)} %constant.14.clone.constants_hbm.constants_ref), custom_call_target="tpu_custom_call" | custom-call | tf_op jit(solution)/shard_map/front/pallas_call | solution.py:371
  38.3 12.5 %all_to_all.46 = bf16[32,16,256]{2,1,0:T(8,128)(2,1)S(1)} all-to-all(bf16[32,16,256]{2,1,0:T(8,128)(2,1)S(1)} %bitcast.21), channel_id=1, replica_groups=mesh['ctx'=32,'tp'=8] {'ctx'}, dimensions={0} | all-to-all | bytes 524288 | tf_op jit(solution)/shard_map/all_to_all | solution.py:359
  50.8 0.0 copy-done.3
  50.8 2.7 %convolution_convert_fusion = bf16[256,4096]{1,0:T(8,128)(2,1)} fusion(bf16[512,256]{1,0:T(8,128)(2,1)S(1)} %bitcast.24, bf16[512,4096]{1,0:T(8,128)(2,1)S(1)} %copy-done.3), kind=kOutput, calls=%fused_computation | convolution fusion | flops 1074790400 | bytes 6553600 | tf_op jit(solution)/shard_map/dot_general | solution.py:388
  53.5 0.0 reduce-scatter.2.cloned.1.call-update
  53.5 0.0 all-gather.2.cloned.1.call-done
  53.5 0.0 copy-start.1
  53.5 0.0 copy-start.2
  53.6 4.3 %convolution_convert_fusion.1 = bf16[512,256]{1,0:T(8,128)(2,1)S(1)} fusion(bf16[512,4096]{1,0:T(8,128)(2,1)} %param.9, bf16[256,4096]{1,0:T(8,128)(2,1)} %all-gather.2.cloned.1.call-done), kind=kOutput, calls=%fused_computation.1 | convolution fusion | flops 1073872896 | bytes 6553600 | tf_op jit(solution)/shard_map/dot_general | solution.py:393
  57.8 17.6 %all_to_all.47 = bf16[32,16,256]{2,1,0:T(8,128)(2,1)S(1)} all-to-all(bf16[32,16,256]{2,1,0:T(8,128)(2,1)S(1)} %bitcast.25), channel_id=1, replica_groups=mesh['ctx'=32,'tp'=8] {'ctx'}, dimensions={0} | all-to-all | bytes 524288 | tf_op jit(solution)/shard_map/all_to_all | solution.py:359
  75.4 0.0 copy-done.1
  75.4 0.0 copy-done.2
  75.4 7.5 %back.1 = bf16[512,384]{1,0:T(8,128)(2,1)S(1)} custom-call(bf16[512,256]{1,0:T(8,128)(2,1)S(1)} %bitcast.20, bf16[3136,512]{1,0:T(8,128)(2,1)S(1)} %copy-done.1, bf16[512,896]{1,0:T(8,128)(2,1)S(1)} %get-tuple-element.17.parts_ref, f32[512,1280]{1,0:T(8,128)S(1)} %copy-done.2), custom_call_target="tpu_custom_call" | custom-call | tf_op jit(solution)/shard_map/back/pallas_call | solution.py:397
  82.9 13.7 %all_to_all.48 = bf16[32,16,384]{2,1,0:T(8,128)(2,1)S(1)} all-to-all(bf16[32,16,384]{2,1,0:T(8,128)(2,1)S(1)} %bitcast.17), channel_id=1, replica_groups=mesh['ctx'=32,'tp'=8] {'ctx'}, dimensions={0} | all-to-all | bytes 786432 | tf_op jit(solution)/shard_map/all_to_all | solution.py:359
  96.6 1.7 %finish.1 = (f32[256,512]{1,0:T(8,128)}, f32[3,16,512]{2,1,0:T(8,128)}) custom-call(bf16[512,384]{1,0:T(8,128)(2,1)S(1)} %bitcast.19), custom_call_target="tpu_custom_call" | custom-call | tf_op jit(solution)/shard_map/finish/pallas_call | solution.py:411
  (2 shorter events, 0.0 us)
Async XLA Ops:
  7.2 2.7 %copy-start = (bf16[512,3,512]{2,0,1:T(8,128)(2,1)S(1)}, bf16[512,3,512]{2,0,1:T(8,128)(2,1)}, u32[]{:S(2)}) copy-start(bf16[512,3,512]{2,0,1:T(8,128)(2,1)} %param.7) | copy-start | bytes 4718596
  7.2 46.3 %all-gather.2.cloned.1.call-start = ((), (), s32[]{:S(2)}) async-start(), calls=%async_computation.6 | async-start | bytes 2359296 | tf_op jit(solution)/shard_map/all_gather | solution.py:369
  7.9 90.4 %reduce-scatter.2.cloned.1.call-start = ((), (), s32[]{:S(2)}) async-start(), calls=%async_computation.5 | async-start | bytes 2359296 | tf_op jit(solution)/shard_map/reduce_scatter | solution.py:391
  10.2 40.6 %copy-start.3 = (bf16[512,4096]{1,0:T(8,128)(2,1)S(1)}, bf16[512,4096]{1,0:T(8,128)(2,1)}, u32[]{:S(2)}) copy-start(bf16[512,4096]{1,0:T(8,128)(2,1)} %param.9) | copy-start | bytes 12582916
  53.5 21.9 %copy-start.1 = (bf16[3136,512]{1,0:T(8,128)(2,1)S(1)}, bf16[3136,512]{1,0:T(8,128)(2,1)}, u32[]{:S(2)}) copy-start(bf16[3136,512]{1,0:T(8,128)(2,1)} %constant.14.clone.constants_hbm.constants_ref) | copy-start | bytes 9633796
  53.5 21.9 %copy-start.2 = (f32[512,1280]{1,0:T(8,128)S(1)}, f32[512,1280]{1,0:T(8,128)}, u32[]{:S(2)}) copy-start(f32[512,1280]{1,0:T(8,128)} %get-tuple-element.18.spectra_ref) | copy-start | bytes 7864324
Sparse Core Ops, SparseCore 0:
  9.8 41.2 all-gather.1
  54.2 40.2 reduce-scatter.1
